TPU v7x, 512 devices: a whole 4x8x8 slice. The times are simulated.
512 devices in a mesh: dp: 128 (over z, y, core), group: 4 (over x).
Axes of the slice: x: 4, y: 8, z: 8, core: 2. Of those that a mesh axis runs over, the one named last changes fastest.
Arguments:
- tokens: bfloat16 [81920, 1280], P('dp', 'group'), may hold values from -40 to 40
- cotangent: bfloat16 [81920, 1280], P('dp', 'group'), may hold values from -6 to 6
- slot_table: int32 [640, 2], replicated, may hold values from -1 to 128, as said below
- w_qkv: bfloat16 [1280, 1920], P(None, 'group'), may hold values from -0.15625 to 0.15625
- qkv_bias: float32 [1920], P('group'), may hold values from -3 to 3
- w_out: bfloat16 [640, 1280], P('group'), may hold values from -0.625 to 0.625
- out_bias: float32 [1280], P('group'), may hold values from -3 to 3
Outputs:
- layer_out: bfloat16 [81920, 1280], P('dp', 'group')
- input_grad: bfloat16 [81920, 1280], P('dp', 'group')
- w_qkv_grad: bfloat16 [1280, 1920], P(None, 'group')
- qkv_bias_grad: float32 [1920], P('group')
- w_out_grad: bfloat16 [640, 1280], P('group')
- out_bias_grad: float32 [1280], P('group')
Inputs may be any that keep to these rules, and one draw needn't show every extreme that they name: `slot_table`: column 0 is the patch count of each home image slot of each dp index: 0 for an empty slot, else 128/4 to 128. Column 1 says where the image is processed: p below 3 means on its own dp index in processing slot p; 3 + p, with p below 2, means on the dp index half the axis away, in that index's processing slot p; -1 for an empty slot. Every dp index holds 1 to 5 images and every processing slot of every dp index receives exactly one image. Only an index holding more than 3 images sends images away, at most 2 of them, and its partner then holds fewer than 3.
All inputs are finite; a program needn't handle non-finite values.
Results may differ from a plain program's by a relative error of at most 0.027.
The roundings to bfloat16 on the way count: a program that leaves them out, or rounds other values in their place, can miss the bound.
Values may be sent and summed in bfloat16 or wider, within the bound.
A program may use at most 64 MiB of HBM per device.

v0:
```python
import math

import jax
import jax.numpy as jnp
from jax import lax
from jax.sharding import PartitionSpec as P

HD = 80
IMG = 128


def layer_pass(work_x, work_g, work_count, w_qkv, qkv_bias, w_out, out_bias, grad_scale):
    slot_count = work_x.shape[0]
    feat_width = work_x.shape[2]
    row_count = slot_count * IMG
    heads_here = w_out.shape[0] // HD
    row_valid = jnp.arange(IMG)[None, :] < work_count[:, None]
    mask_rows = row_valid.reshape(row_count, 1)
    local_x = work_x.reshape(row_count, feat_width)
    local_g = work_g.reshape(row_count, feat_width)
    full_x, full_g = (
        lax.all_gather(local_x, "group", axis=1, tiled=True),
        lax.all_gather(local_g, "group", axis=1, tiled=True),
    )
    projected = jnp.dot(full_x, w_qkv, preferred_element_type=jnp.float32) + qkv_bias
    projected = projected.astype(jnp.bfloat16).reshape(slot_count, IMG, heads_here, 3, HD)
    queries = projected[:, :, :, 0]
    key_rows = projected[:, :, :, 1]
    values = projected[:, :, :, 2]
    score_scale = 1.0 / math.sqrt(HD)
    scores = (
        jnp.einsum("sihe,sjhe->shij", queries, key_rows, preferred_element_type=jnp.float32)
        * score_scale
    )
    scores = jnp.where(row_valid[:, None, None, :], scores, -1e30)
    row_top = jnp.max(scores, axis=-1, keepdims=True)
    exponent = jnp.exp(scores - row_top)
    attn_probs = exponent / jnp.sum(exponent, axis=-1, keepdims=True)
    probs_b = attn_probs.astype(jnp.bfloat16)
    mixed = jnp.einsum("shij,sjhe->sihe", probs_b, values, preferred_element_type=jnp.float32)
    mixed = mixed.astype(jnp.bfloat16).reshape(row_count, heads_here * HD)
    out_term = jnp.dot(mixed, w_out, preferred_element_type=jnp.float32)
    branch = lax.psum_scatter(
        out_term.astype(jnp.bfloat16), "group", scatter_dimension=1, tiled=True
    ).astype(jnp.float32)
    layer_out = jnp.where(mask_rows, local_x.astype(jnp.float32) + branch + out_bias, 0.0).astype(
        jnp.bfloat16
    )
    grad_mixed = jnp.einsum("rd,cd->rc", full_g, w_out, preferred_element_type=jnp.float32)
    grad_mixed = grad_mixed.astype(jnp.bfloat16).reshape(slot_count, IMG, heads_here, HD)
    w_out_grad = jnp.einsum("rc,rd->cd", mixed, full_g, preferred_element_type=jnp.float32)
    out_bias_grad = jnp.sum(local_g.astype(jnp.float32), axis=0)
    grad_probs = jnp.einsum(
        "sihe,sjhe->shij", grad_mixed, values, preferred_element_type=jnp.float32
    )
    inner = jnp.sum(attn_probs * grad_probs, axis=-1, keepdims=True)
    grad_scores = (attn_probs * (grad_probs - inner) * score_scale).astype(jnp.bfloat16)
    grad_query = jnp.einsum(
        "shij,sjhe->sihe", grad_scores, key_rows, preferred_element_type=jnp.float32
    )
    grad_keys = jnp.einsum(
        "shij,sihe->sjhe", grad_scores, queries, preferred_element_type=jnp.float32
    )
    grad_values = jnp.einsum(
        "shij,sihe->sjhe", probs_b, grad_mixed, preferred_element_type=jnp.float32
    )
    grad_proj = jnp.stack([grad_query, grad_keys, grad_values], axis=3).reshape(
        row_count, heads_here * 3 * HD
    )
    qkv_bias_grad = jnp.sum(grad_proj, axis=0)
    grad_proj_b = grad_proj.astype(jnp.bfloat16)
    w_qkv_grad = jnp.einsum("rd,rc->dc", full_x, grad_proj_b, preferred_element_type=jnp.float32)
    input_term = jnp.einsum("rc,dc->rd", grad_proj_b, w_qkv, preferred_element_type=jnp.float32)
    input_sum = lax.psum_scatter(
        input_term.astype(jnp.bfloat16), "group", scatter_dimension=1, tiled=True
    ).astype(jnp.float32)
    input_grad = jnp.where(mask_rows, local_g.astype(jnp.float32) + input_sum, 0.0).astype(
        jnp.bfloat16
    )
    w_qkv_grad, qkv_bias_grad, w_out_grad, out_bias_grad = lax.psum(
        (w_qkv_grad, qkv_bias_grad, w_out_grad, out_bias_grad), "dp"
    )
    grads = (
        (w_qkv_grad * grad_scale).astype(jnp.bfloat16),
        qkv_bias_grad * grad_scale,
        (w_out_grad * grad_scale).astype(jnp.bfloat16),
        out_bias_grad * grad_scale,
    )
    outputs = jnp.stack(
        [
            layer_out.reshape(slot_count, IMG, feat_width),
            input_grad.reshape(slot_count, IMG, feat_width),
        ]
    )
    return (outputs, grads)


def local(tokens, cotangent, slot_table, w_qkv, qkv_bias, w_out, out_bias):
    dp_count = lax.axis_size("dp")
    own_index = lax.axis_index("dp")
    home_slots = slot_table.shape[0] // dp_count
    feat_width = tokens.shape[1]
    grad_scale = 1.0 / math.sqrt(dp_count * home_slots * IMG)
    slot_counts = slot_table[:, 0].reshape(dp_count, home_slots)
    own_count = lax.dynamic_index_in_dim(slot_counts, own_index, 0, keepdims=False)
    home_valid = jnp.arange(IMG)[None, :] < own_count[:, None]
    home_x = tokens.reshape(home_slots, IMG, feat_width)
    home_g = jnp.where(
        home_valid[:, :, None],
        cotangent.reshape(home_slots, IMG, feat_width),
        jnp.zeros((), jnp.bfloat16),
    )
    home_out, grads = layer_pass(
        home_x, home_g, own_count, w_qkv, qkv_bias, w_out, out_bias, grad_scale
    )
    layer_out = home_out[0].reshape(home_slots * IMG, feat_width)
    input_grad = home_out[1].reshape(home_slots * IMG, feat_width)
    return (layer_out, input_grad, grads[0], grads[1], grads[2], grads[3])


def solution(mesh):
    return jax.shard_map(
        local,
        mesh=mesh,
        in_specs=(
            P("dp", "group"),
            P("dp", "group"),
            P(),
            P(None, "group"),
            P("group"),
            P("group", None),
            P("group"),
        ),
        out_specs=(
            P("dp", "group"),
            P("dp", "group"),
            P(None, "group"),
            P("group"),
            P("group", None),
            P("group"),
        ),
        check_vma=False,
    )
```

profile of v0, /device:TPU:1, one launch (start us, length us, event | category | flops | bytes accessed | tf_op | source)
XLA Modules:
  0.0 381.2 jit_solution(1671605411928657641)
XLA Ops:
  7.2 0.0 copy-start
  7.2 0.0 copy-start.7
  7.2 0.0 all-gather.5.cloned.1.call-start
  7.2 0.8 slice_reduce_fusion
  8.1 0.2 reshape_squeeze.3
  8.3 0.1 fusion.42
  8.4 1.8 convert_reduce_fusion
  10.2 0.0 all-gather.5.cloned.1.call-update
  10.3 0.0 all-gather.3.cloned.1.call-start
  10.3 0.7 all-gather.3.cloned.1.call-update
  11.0 0.0 all-reduce.4.cloned.1.call-start
  11.1 37.5 %all-gather.5.cloned.1.call-done = bf16[640,1280]{0,1:T(8,128)(2,1)} async-done(((bf16[640,320]{0,1:T(8,128)(2,1)}), bf16[640,1280]{0,1:T(8,128)(2,1)}) %all-gather.5.cloned.1.call-update) | async-done | bytes 1638416 | tf_op jit(solution)/shard_map/all_gather | solution.py:23
  48.6 1.9 convolution_convert_fusion.2
  50.5 0.2 reshape.89
  50.8 32.3 %all-gather.3.cloned.1.call-done = bf16[640,1280]{0,1:T(8,128)(2,1)} async-done(((bf16[640,320]{0,1:T(8,128)(2,1)}), bf16[640,1280]{0,1:T(8,128)(2,1)}) %all-gather.3.cloned.1.call-update) | async-done | bytes 1638416 | tf_op jit(solution)/shard_map/all_gather | solution.py:22
  83.1 2.6 fusion.3
  85.7 0.7 reshape.87
  86.4 0.9 fusion.43
  87.3 0.3 fusion.30
  87.6 2.2 fusion.44
  89.8 2.0 fusion.10
  91.8 1.8 convolution_bitcast_fusion.3
  93.7 1.7 convolution_bitcast_fusion.2
  95.4 1.5 convolution_bitcast_fusion.1
  96.9 0.1 copy.37
  97.0 0.6 copy-done.4
  97.7 0.1 fusion.12
  97.8 0.3 copy.43
  98.1 1.0 copy-done.1
  99.1 1.5 fusion.25
  100.6 2.6 convolution_bitcast_fusion
  103.3 0.0 all-reduce.4.cloned.1.call-update
  103.3 0.0 reduce-scatter.5.cloned.1.call-start
  103.3 2.5 convolution_convert_fusion.1
  105.8 0.0 reduce-scatter.5.cloned.1.call-update
  105.8 0.0 reduce-scatter.3.cloned.1.call-start
  105.9 0.9 copy-done.8
  106.8 1.9 convolution_convert_fusion
  108.7 0.0 reduce-scatter.3.cloned.1.call-update
  108.7 0.2 fusion.11
  108.9 0.1 reduce_sum.41
  109.0 248.5 %all-reduce = (f32[480]{0:T(512)S(1)}, f32[320]{0:T(512)S(1)}) all-reduce(f32[480]{0:T(512)S(1)} %reduce_sum.41, f32[320]{0:T(512)S(1)} %get-tuple-element.10), channel_id=1, replica_groups=mesh['dp'=128,'group'=4] {'dp'}, use_global_device_ids=true, to_apply=%region_7.8 | all-reduce | flops 800 | bytes 6400 | tf_op jit(solution)/shard_map/psum | solution.py:80
  357.5 0.6 broadcast_multiply_fusion.1
  358.1 0.6 broadcast_multiply_fusion
  358.7 2.0 multiply_convert_fusion.1
  360.6 3.0 multiply_convert_fusion
  363.7 8.9 %reduce-scatter.3.cloned.1.call-done = bf16[640,320]{0,1:T(8,128)(2,1)} async-done(((bf16[640,1280]{0,1:T(8,128)(2,1)}), bf16[640,320]{0,1:T(8,128)(2,1)}) %reduce-scatter.3.cloned.1.call-update) | async-done | bytes 409616 | tf_op jit(solution)/shard_map/reduce_scatter | solution.py:43
  372.5 2.2 fusion.14
  (27 shorter events, 0.1 us)
Async XLA Ops:
  7.2 76.0 %copy-start = (bf16[1280,480]{0,1:T(8,128)(2,1)S(1)}, bf16[1280,480]{0,1:T(8,128)(2,1)}, u32[]{:S(2)}) copy-start(bf16[1280,480]{0,1:T(8,128)(2,1)} %param.10) | copy-start | bytes 3686404
  7.2 41.4 %copy-start.7 = (bf16[160,1280]{1,0:T(8,128)(2,1)S(1)}, bf16[160,1280]{1,0:T(8,128)(2,1)}, u32[]{:S(2)}) copy-start(bf16[160,1280]{1,0:T(8,128)(2,1)} %param.12) | copy-start | bytes 1228804
  7.2 41.4 %all-gather.5.cloned.1.call-start = ((), (), s32[]{:S(2)}) async-start(), calls=%async_computation.4 | async-start | bytes 2048000 | tf_op jit(solution)/shard_map/all_gather | solution.py:23
  10.2 72.9 %copy-start.13 = (f32[480]{0:T(512)S(1)}, f32[480]{0:T(512)}, u32[]{:S(2)}) copy-start(f32[480]{0:T(512)} %param.11) | copy-start | bytes 5764
  10.3 72.9 %all-gather.3.cloned.1.call-start = ((), (), s32[]{:S(2)}) async-start(), calls=%async_computation.2 | async-start | bytes 2048000 | tf_op jit(solution)/shard_map/all_gather | solution.py:22
  11.0 347.7 %all-reduce.4.cloned.1.call-start = ((), (), s32[]{:S(2)}) async-start(), calls=%async_computation.6 | async-start | bytes 6553600 | tf_op jit(solution)/shard_map/psum | solution.py:80
  87.3 2.5 copy-start.9
  91.8 1.8 copy-start.10
  95.4 1.5 copy-start.11
  96.9 0.8 copy-start.4
  97.7 1.4 copy-start.1
  98.1 2.5 copy-start.3
  103.3 260.4 %reduce-scatter.5.cloned.1.call-start = ((), (), s32[]{:S(2)}) async-start(), calls=%async_computation.5 | async-start | bytes 2048000 | tf_op jit(solution)/shard_map/reduce_scatter | solution.py:74
  105.8 1.0 copy-start.8
  105.8 2.9 copy-start.5
  105.8 266.7 %reduce-scatter.3.cloned.1.call-start = ((), (), s32[]{:S(2)}) async-start(), calls=%async_computation.3 | async-start | bytes 2048000 | tf_op jit(solution)/shard_map/reduce_scatter | solution.py:43
  360.6 11.9 %copy-start.2 = (bf16[640,320]{0,1:T(8,128)(2,1)S(1)}, bf16[640,320]{0,1:T(8,128)(2,1)}, u32[]{:S(2)}) copy-start(bf16[640,320]{0,1:T(8,128)(2,1)} %get-tuple-element.11) | copy-start | bytes 1228804
  360.6 11.9 %copy-start.6 = (bf16[640,320]{0,1:T(8,128)(2,1)S(1)}, bf16[640,320]{0,1:T(8,128)(2,1)}, u32[]{:S(2)}) copy-start(bf16[640,320]{0,1:T(8,128)(2,1)} %param.7) | copy-start | bytes 1228804
  360.6 11.9 %copy-start.12 = (f32[320]{0:T(512)S(1)}, f32[320]{0:T(512)}, u32[]{:S(2)}) copy-start(f32[320]{0:T(512)} %param.13) | copy-start | bytes 3844
Sparse Core Ops, SparseCore 0:
  10.7 37.8 all-gather.4
  50.7 32.3 all-gather.2
  103.4 203.2 all-reduce.3
  309.4 29.0 reduce-scatter.4
  341.4 31.0 reduce-scatter.2
where the time goes:
time: 382 us; the launch traced here: 381 us
  blocking collectives  248 us (65%)
  waiting for transfers between devices  79.5 us (21%)
  matrix products  22.6 us (6%)
  between operations  13.9 us (4%)
  other arithmetic  10.5 us (3%)
  local copies, waits for them, and re-layouts  6 us (2%)
    psum x1, blocking collectives, layer_pass(): lax.psum((w_qkv_grad, qkv_bias_grad, w_out_grad, out_bias_grad), 'dp')  248 us
    all_gather x1, waiting for transfers between devices, layer_pass(): lax.all_gather(local_g, 'group', axis=1, tiled=True)  37.5 us
    all_gather x1, waiting for transfers between devices, layer_pass(): lax.all_gather(local_x, 'group', axis=1, tiled=True)  32.3 us
    reduce_scatter x1, waiting for transfers between devices, layer_pass(): lax.psum_scatter(out_term.astype(jnp.bfloat16), 'group', scatter_dimensio...  8.87 us
  transfers between devices with their start and end apart: 5, of which 3 were waited for; matrix products, arithmetic and copies ran while one was open for 3% of the time, Pallas kernels for 0%

commit v1 on v0

v1 whole, which is shorter than its diff:
```python
import functools
import math

import jax
import jax.numpy as jnp
from jax import lax
from jax.experimental import pallas as pl
from jax.experimental.pallas import tpu as pltpu
from jax.sharding import PartitionSpec as P

HD = 80
IMG = 128
MESH = pl.DeviceIdType.MESH
BF16 = jnp.bfloat16
F32 = jnp.float32


def far_first(n):
    return sorted(range(1, n), key=lambda k: (-min(k, n - k), k))


def comm_kernel(
    n, nb, nb2, slots, scale,
    cnt_ref, op_ref, ip_ref, g_ref, x_ref, gi_ref, bias_ref,
    lo_ref, ig_ref, f_ref,
    r0, s1, r1, t, r2, v, fw, mrg, rcv,
    b0s, b0r, b1s, b1r, b2s, b2r, b3s, b3r, b4s, b4r, b5s, b5r,
    xs, xr,
):
    dp = lax.axis_index("dp")
    grp = lax.axis_index("group")
    c = lax.rem(dp, 2)
    y = lax.rem(lax.div(dp, 2), n)
    z = lax.div(dp, 2 * n)
    other = dp + 1 - 2 * c
    gr = lax.rem(grp + 1, 4)
    gl = lax.rem(grp + 3, 4)
    me = (y, z)

    def on_axis(axis, idx):
        return (z * n + idx) * 2 + c if axis == 0 else (idx * n + y) * 2 + c

    def plus(a, k):
        return lax.rem(a + k, n)

    def send(src, dst, ss, rs, d, g):
        return pltpu.make_async_remote_copy(
            src_ref=src, dst_ref=dst, send_sem=ss, recv_sem=rs,
            device_id=(d, g), device_id_type=MESH,
        )

    barrier = pltpu.get_barrier_semaphore()
    pl.semaphore_signal(barrier, inc=1, device_id=(other, grp), device_id_type=MESH)
    for axis in (0, 1):
        for k in range(1, n):
            pl.semaphore_signal(
                barrier, inc=1, device_id=(on_axis(axis, plus(me[axis], k)), grp),
                device_id_type=MESH,
            )
    for g in (gr, gl):
        pl.semaphore_signal(barrier, inc=1, device_id=(dp, g), device_id_type=MESH)
    pl.semaphore_wait(barrier, 1 + 2 * (n - 1) + 2)

    order = far_first(n) + [0]

    def l0(s, k):
        p = plus(me[s], k)
        return send(g_ref.at[1 - c, s, p], r0.at[s, p], b0s.at[s, k], b0r.at[s, k], other, grp)

    for k in order:
        for s in (0, 1):
            l0(s, k).start()

    half = IMG // 2
    gx = lax.rem(grp + 2, 4)

    def x_copy(arr, img, j):
        src = (op_ref, ip_ref)[arr]
        ch = arr * slots + img
        lo = pl.ds(img * IMG, half)
        hi = pl.ds(img * IMG + half, half)
        return (
            lambda: send(src.at[gx, lo], fw.at[ch, 0], xs.at[ch, 0], xr.at[ch, 0], dp, gr),
            lambda: send(src.at[gx, hi], fw.at[ch, 1], xs.at[ch, 1], xr.at[ch, 1], dp, gl),
            lambda: send(src.at[gr, hi], rcv.at[ch, 0, 1], xs.at[ch, 2], xr.at[ch, 2], dp, gr),
            lambda: send(src.at[gl, lo], rcv.at[ch, 1, 0], xs.at[ch, 3], xr.at[ch, 3], dp, gl),
            lambda: send(mrg.at[ch, 0], rcv.at[ch, 0, 0], xs.at[ch, 4], xr.at[ch, 4], dp, gr),
            lambda: send(mrg.at[ch, 1], rcv.at[ch, 1, 1], xs.at[ch, 5], xr.at[ch, 5], dp, gl),
        )[j]()

    for arr in (0, 1):
        def raw(img, _, arr=arr):
            for j in range(4):
                x_copy(arr, img, j).start()
            return 0
        lax.fori_loop(0, slots, raw, 0)

    def l1(s, k):
        return send(
            s1.at[s, k], r1.at[s, k], b1s.at[s, k], b1r.at[s, k],
            on_axis(s, plus(me[s], k)), grp,
        )

    for k in order:
        for s in (0, 1):
            l0(s, k).wait_recv()
            p = plus(me[s], k)
            total = g_ref[c, s, p] + r0[s, p]
            if k:
                s1[s, k] = total.astype(BF16)
                l1(s, k).start()
            else:
                t[s, pl.ds(0, nb)] = total
                if nb2 * n > nb:
                    t[s, pl.ds(nb, nb2 * n - nb)] = jnp.zeros((nb2 * n - nb, 16, 128), F32)

    def merge(arr):
        def step(img, _):
            ch = arr * slots + img
            src = (op_ref, ip_ref)[arr]
            x_copy(arr, img, 0).wait_recv()
            mine = src[gr, pl.ds(img * IMG, half)].astype(F32)
            mrg[ch, 0] = (mine + fw[ch, 0].astype(F32)).astype(BF16)
            x_copy(arr, img, 4).start()
            x_copy(arr, img, 1).wait_recv()
            mine = src[gl, pl.ds(img * IMG + half, half)].astype(F32)
            mrg[ch, 1] = (mine + fw[ch, 1].astype(F32)).astype(BF16)
            x_copy(arr, img, 5).start()
            return 0
        lax.fori_loop(0, slots, step, 0)

    merge(0)

    def l2(s, k):
        q = plus(me[1 - s], k)
        return send(
            t.at[s, pl.ds(q * nb2, nb2)], r2.at[s, k], b2s.at[s, k], b2r.at[s, k],
            on_axis(1 - s, q), grp,
        )

    near = list(reversed(far_first(n)))
    for s in (0, 1):
        for k in near:
            l1(s, k).wait_recv()
        total = t[s, pl.ds(0, nb)]
        for k in near:
            total = total + r1[s, k].astype(F32)
        t[s, pl.ds(0, nb)] = total
        for k in far_first(n):
            l2(s, k).start()

    merge(1)

    def l3(s, k):
        mine = v.at[s, pl.ds(me[1 - s] * nb2, nb2)]
        return send(
            mine, mine, b3s.at[s, k], b3r.at[s, k], on_axis(1 - s, plus(me[1 - s], k)), grp,
        )

    for s in (0, 1):
        for k in near:
            l2(s, k).wait_recv()
        total = t[s, pl.ds(me[1 - s] * nb2, nb2)]
        for k in near:
            total = total + r2[s, k]
        v[s, pl.ds(me[1 - s] * nb2, nb2)] = (total * scale).astype(BF16)
        for k in far_first(n):
            l3(s, k).start()

    def l4(s, k):
        return send(
            v.at[s, pl.ds(0, nb)], f_ref.at[c, s, me[s]], b4s.at[s, k], b4r.at[s, k],
            on_axis(s, plus(me[s], k)), grp,
        )

    def l5(s, k):
        piece = f_ref.at[c, s, plus(me[s], k)]
        return send(piece, piece, b5s.at[s, k], b5r.at[s, k], other, grp)

    def l3_in(s, k):
        src = v.at[s, pl.ds(plus(me[1 - s], n - k) * nb2, nb2)]
        return send(src, src, b3s.at[s, k], b3r.at[s, k], other, grp)

    for s in (0, 1):
        for k in near:
            l3_in(s, k).wait_recv()
        for k in far_first(n):
            l4(s, k).start()
        f_ref[c, s, me[s]] = v[s, pl.ds(0, nb)]
        l5(s, 0).start()

    def l4_in(s, k):
        dst = f_ref.at[c, s, plus(me[s], n - k)]
        return send(dst, dst, b4s.at[s, k], b4r.at[s, k], other, grp)

    for k in near:
        for s in (0, 1):
            l4_in(s, k).wait_recv()
            l5(s, n - k).start()

    def finish(arr):
        def step(img, _):
            ch = arr * slots + img
            for j in range(2, 6):
                x_copy(arr, img, j).wait_recv()
            rows_at = pl.ds(img * IMG, IMG)
            src = (op_ref, ip_ref)[arr]
            total = src[grp, rows_at].astype(F32)
            total = total + rcv[ch, 0].reshape(IMG, -1).astype(F32)
            total = total + rcv[ch, 1].reshape(IMG, -1).astype(F32)
            if arr == 0:
                total = total + x_ref[rows_at].astype(F32) + bias_ref[...]
            else:
                total = total + gi_ref[rows_at].astype(F32)
            row = lax.broadcasted_iota(jnp.int32, total.shape, 0)
            total = jnp.where(row < cnt_ref[img], total, 0.0).astype(BF16)
            (lo_ref, ig_ref)[arr][rows_at] = total
            return 0
        lax.fori_loop(0, slots, step, 0)

    finish(0)
    finish(1)

    def l5_in(s, k):
        piece = f_ref.at[1 - c, s, plus(me[s], k)]
        return send(piece, piece, b5s.at[s, k], b5r.at[s, k], other, grp)

    for k in range(n):
        for s in (0, 1):
            l5_in(s, k).wait_recv()
            l0(s, k).wait_send()
            l5(s, k).wait_send()
            if k:
                l1(s, k).wait_send()
                l2(s, k).wait_send()
                l3(s, k).wait_send()
                l4(s, k).wait_send()
    for arr in (0, 1):
        def done(img, _, arr=arr):
            for j in range(6):
                x_copy(arr, img, j).wait_send()
            return 0
        lax.fori_loop(0, slots, done, 0)


def reduce_all(n, slots, scale, cnt, out_parts, in_parts, grads, x, gi, bias):
    nb = grads.shape[3]
    nb2 = -(-nb // n)
    rows, width = x.shape
    vm = pl.BlockSpec(memory_space=pltpu.VMEM)
    dma = pltpu.SemaphoreType.DMA
    chunks = 2 * slots
    return pl.pallas_call(
        functools.partial(comm_kernel, n, nb, nb2, slots, scale),
        out_shape=(
            jax.ShapeDtypeStruct((rows, width), BF16),
            jax.ShapeDtypeStruct((rows, width), BF16),
            jax.ShapeDtypeStruct((2, 2, n, nb, 16, 128), BF16),
        ),
        in_specs=[pl.BlockSpec(memory_space=pltpu.SMEM)] + [vm] * 6,
        out_specs=(vm, vm, vm),
        scratch_shapes=[
            pltpu.VMEM((2, n, nb, 16, 128), F32),
            pltpu.VMEM((2, n, nb, 16, 128), BF16),
            pltpu.VMEM((2, n, nb, 16, 128), BF16),
            pltpu.VMEM((2, n * nb2, 16, 128), F32),
            pltpu.VMEM((2, n, nb2, 16, 128), F32),
            pltpu.VMEM((2, n * nb2, 16, 128), BF16),
            pltpu.VMEM((chunks, 2, IMG // 2, width), BF16),
            pltpu.VMEM((chunks, 2, IMG // 2, width), BF16),
            pltpu.VMEM((chunks, 2, 2, IMG // 2, width), BF16),
        ] + [dma((2, n))] * 12 + [dma((chunks, 6))] * 2,
        compiler_params=pltpu.CompilerParams(
            collective_id=0, has_side_effects=True, vmem_limit_bytes=50 * 2**20,
        ),
        cost_estimate=pl.CostEstimate(flops=10**6, bytes_accessed=10**7, transcendentals=0),
    )(cnt, out_parts, in_parts, grads, x, gi, bias)


def to_blocks(n, w_qkv_grad, w_out_grad, qkv_bias_grad, out_bias_grad):
    rows, cols = w_qkv_grad.shape
    wide = -(-cols // 128) * 128
    a = jnp.pad(w_qkv_grad, ((0, 0), (0, wide - cols)))
    a = a.reshape(rows // 16, 16, wide // 128, 128).transpose(0, 2, 1, 3).reshape(-1, 16, 128)
    r2, c2 = w_out_grad.shape
    b = w_out_grad.reshape(r2 // 16, 16, c2 // 128, 128).transpose(0, 2, 1, 3).reshape(-1, 16, 128)
    bias = jnp.concatenate([qkv_bias_grad, out_bias_grad])
    bias = jnp.pad(bias, (0, 2048 - bias.shape[0])).reshape(1, 16, 128)
    used = a.shape[0] + b.shape[0] + 1
    nb = -(-used // (4 * n))
    full = jnp.concatenate([a, b, bias, jnp.zeros((4 * n * nb - used, 16, 128), F32)])
    return full.reshape(2, 2, n, nb, 16, 128)


def from_blocks(full, rows, cols, r2, c2, nq, no):
    full = full.reshape(-1, 16, 128)
    wide = -(-cols // 128) * 128
    na = rows * wide // 2048
    n_b = r2 * c2 // 2048
    a = full[:na].reshape(rows // 16, wide // 128, 16, 128).transpose(0, 2, 1, 3)
    a = a.reshape(rows, wide)[:, :cols]
    b = full[na:na + n_b].reshape(r2 // 16, c2 // 128, 16, 128).transpose(0, 2, 1, 3).reshape(r2, c2)
    bias = full[na + n_b].reshape(-1).astype(F32)
    return a, b, bias[:nq], bias[nq:nq + no]


def local(tokens, cotangent, slot_table, w_qkv, qkv_bias, w_out, out_bias):
    dp_count = lax.axis_size("dp")
    own_index = lax.axis_index("dp")
    slot_count = slot_table.shape[0] // dp_count
    rows, width = tokens.shape
    n = math.isqrt(dp_count // 2)
    grad_scale = 1.0 / math.sqrt(dp_count * slot_count * IMG)
    slot_counts = slot_table[:, 0].reshape(dp_count, slot_count)
    own_count = lax.dynamic_index_in_dim(slot_counts, own_index, 0, keepdims=False)
    row_valid = jnp.arange(IMG)[None, :] < own_count[:, None]
    mask_rows = row_valid.reshape(rows, 1)
    local_x = tokens
    local_g = jnp.where(mask_rows, cotangent, jnp.zeros((), BF16))
    heads_here = w_out.shape[0] // HD
    full_x = lax.all_gather(local_x, "group", axis=1, tiled=True)
    full_g = lax.all_gather(local_g, "group", axis=1, tiled=True)
    projected = jnp.dot(full_x, w_qkv, preferred_element_type=F32) + qkv_bias
    projected = projected.astype(BF16).reshape(slot_count, IMG, heads_here, 3, HD)
    queries = projected[:, :, :, 0]
    key_rows = projected[:, :, :, 1]
    values = projected[:, :, :, 2]
    score_scale = 1.0 / math.sqrt(HD)
    scores = jnp.einsum("sihe,sjhe->shij", queries, key_rows, preferred_element_type=F32) * score_scale
    scores = jnp.where(row_valid[:, None, None, :], scores, -1e30)
    row_top = jnp.max(scores, axis=-1, keepdims=True)
    exponent = jnp.exp(scores - row_top)
    attn_probs = exponent / jnp.sum(exponent, axis=-1, keepdims=True)
    probs_b = attn_probs.astype(BF16)
    mixed = jnp.einsum("shij,sjhe->sihe", probs_b, values, preferred_element_type=F32)
    mixed = mixed.astype(BF16).reshape(rows, heads_here * HD)
    groups = 4
    out_parts = jnp.dot(mixed, w_out, preferred_element_type=F32).astype(BF16)
    out_parts = out_parts.reshape(rows, groups, width).transpose(1, 0, 2)
    grad_mixed = jnp.einsum("rd,cd->rc", full_g, w_out, preferred_element_type=F32)
    grad_mixed = grad_mixed.astype(BF16).reshape(slot_count, IMG, heads_here, HD)
    w_out_grad = jnp.einsum("rc,rd->cd", mixed, full_g, preferred_element_type=F32)
    out_bias_grad = jnp.sum(local_g.astype(F32), axis=0)
    grad_probs = jnp.einsum("sihe,sjhe->shij", grad_mixed, values, preferred_element_type=F32)
    inner = jnp.sum(attn_probs * grad_probs, axis=-1, keepdims=True)
    grad_scores = (attn_probs * (grad_probs - inner) * score_scale).astype(BF16)
    grad_query = jnp.einsum("shij,sjhe->sihe", grad_scores, key_rows, preferred_element_type=F32)
    grad_keys = jnp.einsum("shij,sihe->sjhe", grad_scores, queries, preferred_element_type=F32)
    grad_values = jnp.einsum("shij,sihe->sjhe", probs_b, grad_mixed, preferred_element_type=F32)
    grad_proj = jnp.stack([grad_query, grad_keys, grad_values], axis=3).reshape(rows, heads_here * 3 * HD)
    qkv_bias_grad = jnp.sum(grad_proj, axis=0)
    grad_proj_b = grad_proj.astype(BF16)
    w_qkv_grad = jnp.einsum("rd,rc->dc", full_x, grad_proj_b, preferred_element_type=F32)
    in_parts = jnp.einsum("rc,dc->rd", grad_proj_b, w_qkv, preferred_element_type=F32).astype(BF16)
    in_parts = in_parts.reshape(rows, groups, width).transpose(1, 0, 2)
    blocks = to_blocks(n, w_qkv_grad, w_out_grad, qkv_bias_grad, out_bias_grad)
    layer_out, input_grad, full = reduce_all(
        n, slot_count, grad_scale, own_count, out_parts, in_parts, blocks,
        local_x, local_g, out_bias.reshape(1, width),
    )
    d, cq = w_qkv.shape
    r2, c2 = w_out.shape
    return (layer_out, input_grad) + reorder(from_blocks(full, d, cq, r2, c2, cq, width))


def reorder(grads):
    return grads[0], grads[2], grads[1], grads[3]


def solution(mesh):
    return jax.shard_map(
        local,
        mesh=mesh,
        in_specs=(
            P("dp", "group"),
            P("dp", "group"),
            P(),
            P(None, "group"),
            P("group"),
            P("group", None),
            P("group"),
        ),
        out_specs=(
            P("dp", "group"),
            P("dp", "group"),
            P(None, "group"),
            P("group"),
            P("group", None),
            P("group"),
        ),
        check_vma=False,
    )
```

time: 382 us -> 217 us (0.57)
  blocking collectives: 248 us -> 0 us
  Pallas kernels: 0 us -> 55.2 us
  local copies, waits for them, and re-layouts: 6 us -> 46.7 us
  waiting for transfers between devices: 79.5 us -> 69.9 us
  other arithmetic: 10.5 us -> 5.61 us
    psum x1 -> x0, blocking collectives: 248 us -> none  [layer_pass(): lax.psum((w_qkv_grad, qkv_bias_grad, w_out_grad, out_bias_grad), 'dp')]
    pallas_call x0 -> x1, Pallas kernels: none -> 55.2 us  [reduce_all(): pl.pallas_call(functools.partial(comm_kernel, n, nb, nb2, slots, scale),...]
    reshape x2 -> x6, local copies, waits for them, and re-layouts: 0.93 us -> 13.4 us  [the longest x1 3.96 us: to_blocks(): a.reshape(rows // 16, 16, wide // 128, 128).transpose(0, 2, 1, 3)]
    reduce_scatter x2 -> x0, waiting for transfers between devices: 8.87 us -> none  [the longest x1 8.87 us: layer_pass(): lax.psum_scatter(out_term.astype(jnp.bfloat16), 'group', scatter_dimensio...]
    unnamed x28 -> x37, local copies, waits for them, and re-layouts: 2.62 us -> 10.2 us
    convert_element_type x2 -> x4, local copies, waits for them, and re-layouts: 0.43 us -> 7.47 us  [the longest x1 3.52 us: local(): jnp.einsum('rc,dc->rd', grad_proj_b, w_qkv, preferred_element_type=F32)]
    convert_element_type x4 -> x2, other arithmetic: 7.23 us -> 1.09 us  [the longest x1 1.09 us: local(): grad_proj_b = grad_proj.astype(BF16)]
    transpose x0 -> x3, local copies, waits for them, and re-layouts: none -> 5.67 us  [the longest x1 3.51 us: to_blocks(): a.reshape(rows // 16, 16, wide // 128, 128).transpose(0, 2, 1, 3)]
  transfers between devices with their start and end apart: 5 -> 2, of which waited for: 3 -> 2; matrix products, arithmetic and copies ran while one was open for 3% -> 1% of each run, Pallas kernels for 0% -> 0%
where the time goes in v1:
time: 217 us; the launch traced here: 216 us
  waiting for transfers between devices  69.9 us (32%)
  Pallas kernels  55.2 us (25%)
  local copies, waits for them, and re-layouts  46.7 us (22%)
  matrix products  24.4 us (11%)
  between operations  14.3 us (7%)
  other arithmetic  5.61 us (3%)
    pallas_call x1, Pallas kernels, reduce_all(): pl.pallas_call(functools.partial(comm_kernel, n, nb, nb2, slots, scale),...  55.2 us
    all_gather x1, waiting for transfers between devices, local(): full_g = lax.all_gather(local_g, 'group', axis=1, tiled=True)  36.9 us
    all_gather x1, waiting for transfers between devices, local(): full_x = lax.all_gather(local_x, 'group', axis=1, tiled=True)  32.3 us
    unnamed x37, local copies, waits for them, and re-layouts  10.2 us
  transfers between devices with their start and end apart: 2, of which 2 were waited for; matrix products, arithmetic and copies ran while one was open for 1% of the time, Pallas kernels for 0%

profile of v1, /device:TPU:1, one launch (start us, length us, event | category | flops | bytes accessed | tf_op | source)
XLA Modules:
  0.0 216.2 jit_solution(2577563562281803344)
XLA Ops:
  7.2 0.8 slice_reduce_fusion
  8.0 0.2 reshape_squeeze.4
  8.3 1.3 copy.84
  9.7 0.2 convert_reduce_fusion
  9.9 1.0 copy.85
  10.9 0.7 all-gather.3.cloned.1.call-update
  11.6 0.3 copy.97.x_ref
  12.0 36.9 %all-gather.5.cloned.1.call-done = bf16[640,1280]{0,1:T(8,128)(2,1)} async-done(((bf16[640,320]{0,1:T(8,128)(2,1)}), bf16[640,1280]{0,1:T(8,128)(2,1)}) %all-gather.5.cloned.1.call-update) | async-done | bytes 1638416 | tf_op jit(solution)/shard_map/all_gather | solution.py:322
  48.9 1.9 convolution_convert_fusion.2
  50.8 0.2 reshape.111
  51.1 32.3 %all-gather.3.cloned.1.call-done = bf16[640,1280]{0,1:T(8,128)(2,1)} async-done(((bf16[640,320]{0,1:T(8,128)(2,1)}), bf16[640,1280]{0,1:T(8,128)(2,1)}) %all-gather.3.cloned.1.call-update) | async-done | bytes 1638416 | tf_op jit(solution)/shard_map/all_gather | solution.py:321
  83.4 3.4 %fusion.3 = bf16[640,480]{0,1:T(8,128)(2,1)} fusion(bf16[1280,480]{0,1:T(8,128)(2,1)S(1)} %copy-done, bf16[640,1280]{0,1:T(8,128)(2,1)} %all-gather.3.cloned.1.call-done, f32[480]{0:T(512)S(1)} %copy-done.12), kind=kOutput, calls=%fused_computation.8 | convolution fusion | flops 787046400 | bytes 3483520 | tf_op jit(solution)/shard_map/dot_general | solution.py:323
  86.8 1.7 reshape.108
  88.5 1.0 fusion.38
  89.5 1.2 fusion.25
  90.7 1.5 fusion.39
  92.2 0.8 copy-done.13
  93.1 1.2 fusion.10
  94.3 2.2 %convolution_bitcast_fusion.3 = f32[5,128,2,1,80]{1,4,2,0,3:T(8,128)S(1)} fusion(f32[5,2,128,128]{2,3,1,0:T(8,128)} %fusion.25, bf16[5,128,2,1,80]{1,0,4,3,2:T(8,128)(2,1)S(1)} %copy-done.10, f32[5,2,128,128]{2,3,1,0:T(8,128)} %copy-done.13, f32[5,2,128]{2,1,0:T(2,128)S(1)} %get-tuple-element.43), kind=kOutput, calls=%fused_computation.20 | convolution fusion | flops 27362688 | bytes 1930240 | tf_op jit(solution)/shard_map/shij,sjhe->sihe/dot_general | solution.py:347
  96.6 2.3 %convolution_bitcast_fusion.2 = f32[5,128,2,1,80]{1,4,2,0,3:T(8,128)S(1)} fusion(f32[5,2,128,128]{2,3,1,0:T(8,128)} %fusion.25, bf16[5,128,2,1,80]{1,0,4,3,2:T(8,128)(2,1)} %get-tuple-element.39, f32[5,2,128,128]{2,3,1,0:T(8,128)} %copy-done.13, f32[5,2,128]{2,1,0:T(2,128)S(1)} %get-tuple-element.43), kind=kOutput, calls=%fused_computation.19 | convolution fusion | flops 27362688 | bytes 1930240 | tf_op jit(solution)/shard_map/shij,sihe->sjhe/dot_general | solution.py:348
  98.9 1.7 convolution_bitcast_fusion.1
  100.6 0.2 fusion.11
  100.8 1.1 fusion.12
  102.1 0.3 copy.91
  102.4 2.2 %convolution_convert_fusion.1 = bf16[640,1280]{1,0:T(8,128)(2,1)} fusion(bf16[1280,480]{0,1:T(8,128)(2,1)S(1)} %copy-done, bf16[60,8,5,128]{3,2,1,0:T(8,128)(2,1)S(1)} %bitcast.137), kind=kOutput, calls=%fused_computation.5 | convolution fusion | flops 787251200 | bytes 3481600 | tf_op jit(solution)/shard_map/rc,dc->rd/dot_general | solution.py:354
  104.7 2.6 %convolution_bitcast_fusion = f32[1280,480]{0,1:T(8,128)} fusion(bf16[640,1280]{0,1:T(8,128)(2,1)S(1)} %copy-done.3, bf16[60,8,5,128]{3,2,1,0:T(8,128)(2,1)S(1)} %bitcast.138), kind=kOutput, calls=%fused_computation.4 | convolution fusion | flops 786432000 | bytes 4710400 | tf_op jit(solution)/shard_map/rd,rc->dc/dot_general | solution.py:353
  107.3 3.2 %copy.111 = f32[1280,480]{1,0:T(8,128)} copy(f32[1280,480]{0,1:T(8,128)} %convolution_bitcast_fusion) | data formatting | bytes 4915200
  110.5 3.5 %pad.8.clone = f32[1280,512]{1,0:T(8,128)} pad(f32[1280,480]{1,0:T(8,128)} %copy.111, f32[]{:T(128)} %constant.23.clone.1), padding=0_0x0_32 | pad | bytes 5079044 | tf_op jit(solution)/shard_map/jit(_pad)/pad | solution.py:283
  114.0 4.0 %reshape.113 = f32[80,16,4,128]{3,2,1,0:T(4,128)} reshape(f32[1280,512]{1,0:T(8,128)} %pad.8.clone) | data formatting | bytes 5242880 | tf_op jit(solution)/shard_map/reshape | solution.py:284
  118.0 3.5 %copy.95 = f32[80,4,16,128]{3,2,1,0:T(8,128)} copy(f32[80,4,16,128]{3,1,2,0:T(4,128)} %bitcast.126) | data formatting | bytes 5242880 | tf_op jit(solution)/shard_map/transpose | solution.py:284
  121.5 3.5 %copy.92 = bf16[640,1280]{0,1:T(8,128)(2,1)} copy(bf16[640,1280]{1,0:T(8,128)(2,1)} %convolution_convert_fusion.1) | data formatting | bytes 3276800 | tf_op jit(solution)/shard_map/convert_element_type | solution.py:354
  125.0 3.8 %copy.93 = bf16[640,4,320]{2,0,1:T(8,128)(2,1)} copy(bf16[640,4,320]{0,2,1:T(8,128)(2,1)} %bitcast.129) | data formatting | bytes 3276800 | tf_op jit(solution)/shard_map/reshape | solution.py:355
  128.8 1.9 convolution_convert_fusion
  130.6 3.5 %copy.82 = bf16[640,1280]{0,1:T(8,128)(2,1)} copy(bf16[640,1280]{1,0:T(8,128)(2,1)} %convolution_convert_fusion) | data formatting | bytes 3276800 | tf_op jit(solution)/shard_map/convert_element_type | solution.py:338
  134.1 3.7 %copy.83 = bf16[640,4,320]{2,0,1:T(8,128)(2,1)} copy(bf16[640,4,320]{0,2,1:T(8,128)(2,1)} %bitcast.130) | data formatting | bytes 3276800 | tf_op jit(solution)/shard_map/reshape | solution.py:339
  137.9 2.2 %fusion.40 = f32[10,16,10,128]{3,1,2,0:T(8,128)S(1)} fusion(bf16[10,16,640,1]{2,1,3,0:T(8,128)(2,1)S(1)} %bitcast.140, bf16[10,128,640,1]{2,1,0,3:T(8,128)(2,1)} %bitcast.131), kind=kOutput, calls=%fused_computation.66 | convolution fusion | flops 262144000 | bytes 2662400 | tf_op jit(solution)/shard_map/rc,rd->cd/dot_general | solution.py:342
  140.2 4.0 %maximum_maximum_fusion = f32[448,16,128]{2,1,0:T(8,128)} fusion(f32[1,16,128]{2,1,0:T(8,128)S(1)} %fusion.28, f32[100,16,128]{2,1,0:T(8,128)S(1)} %bitcast.135, f32[320,16,128]{2,1,0:T(8,128)S(1)} %bitcast.125, f32[448]{0:T(512)S(1)} %pad.13.clone), kind=kLoop, calls=%fused_computation.2 | loop fusion | flops 2752512 | bytes 7120640 | tf_op jit(solution)/shard_map/concatenate | solution.py:291
  144.1 55.2 %shard_map.118 = (bf16[640,320]{1,0:T(8,128)(2,1)S(1)}, bf16[640,320]{1,0:T(8,128)(2,1)S(1)}, bf16[2,2,8,14,16,128]{5,4,3,2,1,0:T(8,128)(2,1)S(1)}) custom-call(s32[5]{0:T(128)S(1)} %dynamic-slice_bitcast_fusion.cnt_ref, bf16[4,640,320]{2,1,0:T(8,128)(2,1)} %bitcast.128, bf16[4,640,320]{2,1,0:T(8,128)(2,1)} %bitcast.127, ...), custom_call_target="tpu_custom_call" | custom-call | flops 1000000 | bytes 10000000 | tf_op jit(solution)/shard_map/pallas_call | solution.py:253
  199.3 0.6 slice.48
  200.0 0.6 slice.46
  200.6 0.8 slice.47
  201.3 1.3 slice.43
  202.6 1.0 copy.100
  203.6 1.0 copy.101
  204.6 2.0 copy.98
  206.6 0.2 copy.152
  206.8 1.5 copy.102
  208.5 0.9 copy.153
  (42 shorter events, 0.8 us)
Async XLA Ops:
  7.2 76.2 %copy-start = (bf16[1280,480]{0,1:T(8,128)(2,1)S(1)}, bf16[1280,480]{0,1:T(8,128)(2,1)}, u32[]{:S(2)}) copy-start(bf16[1280,480]{0,1:T(8,128)(2,1)} %param.10) | copy-start | bytes 3686404
  7.2 41.7 %all-gather.5.cloned.1.call-start = ((), (), s32[]{:S(2)}) async-start(), calls=%async_computation.1 | async-start | bytes 2048000 | tf_op jit(solution)/shard_map/all_gather | solution.py:322
  8.3 3.3 %copy-start.2 = (bf16[640,320]{0,1:T(8,128)(2,1)S(1)}, bf16[640,320]{0,1:T(8,128)(2,1)}, u32[]{:S(2)}) copy-start(bf16[640,320]{0,1:T(8,128)(2,1)} %param.7) | copy-start | bytes 1228804
  9.6 2.3 %copy-start.11 = (f32[320]{0:T(512)S(1)}, f32[320]{0:T(512)}, u32[]{:S(2)}) copy-start(f32[320]{0:T(512)} %param.13) | copy-start | bytes 3844
  9.6 39.3 %copy-start.6 = (bf16[160,1280]{1,0:T(8,128)(2,1)S(1)}, bf16[160,1280]{1,0:T(8,128)(2,1)}, u32[]{:S(2)}) copy-start(bf16[160,1280]{1,0:T(8,128)(2,1)} %param.12) | copy-start | bytes 1228804
  10.9 72.5 %all-gather.3.cloned.1.call-start = ((), (), s32[]{:S(2)}) async-start(), calls=%async_computation | async-start | bytes 2048000 | tf_op jit(solution)/shard_map/all_gather | solution.py:321
  11.6 71.8 %copy-start.12 = (f32[480]{0:T(512)S(1)}, f32[480]{0:T(512)}, u32[]{:S(2)}) copy-start(f32[480]{0:T(512)} %param.11) | copy-start | bytes 5764
  51.1 38.5 %copy-start.8 = (bf16[5,128,2,80]{1,0,3,2:T(8,128)(2,1)}, bf16[5,128,2,80]{1,0,3,2:T(8,128)(2,1)S(1)}, u32[]{:S(2)}) copy-start(bf16[5,128,2,80]{1,0,3,2:T(8,128)(2,1)S(1)} %reshape.111) | copy-start | bytes 614404
  89.5 1.2 copy-start.9
  92.2 0.8 copy-start.13
  92.2 2.1 copy-start.10
  98.9 1.7 copy-start.5
  102.4 2.2 %copy-start.3 = (bf16[640,1280]{0,1:T(8,128)(2,1)S(1)}, bf16[640,1280]{0,1:T(8,128)(2,1)}, u32[]{:S(2)}) copy-start(bf16[640,1280]{0,1:T(8,128)(2,1)} %all-gather.3.cloned.1.call-done) | copy-start | bytes 4915204
  125.0 3.8 %copy-start.7 = (bf16[160,1280]{1,0:T(8,128)(2,1)S(1)}, bf16[160,1280]{1,0:T(8,128)(2,1)}, u32[]{:S(2)}) copy-start(bf16[160,1280]{1,0:T(8,128)(2,1)} %param.12) | copy-start | bytes 1228804
  137.9 2.3 %copy-start.1 = (f32[80,4,16,128]{3,2,1,0:T(8,128)S(1)}, f32[80,4,16,128]{3,2,1,0:T(8,128)}, u32[]{:S(2)}) copy-start(f32[80,4,16,128]{3,2,1,0:T(8,128)} %copy.95) | copy-start | bytes 7864324
  206.8 1.5 copy-start.4
Sparse Core Ops, SparseCore 0:
  11.0 37.8 all-gather.4
  51.0 32.3 all-gather.2

commit v2 on v1

v2 whole, which is shorter than its diff:
```python
import functools
import math

import jax
import jax.numpy as jnp
from jax import lax
from jax.experimental import pallas as pl
from jax.experimental.pallas import tpu as pltpu
from jax.sharding import PartitionSpec as P

HD = 80
IMG = 128
GROUPS = 4
LANES = 128
TILE = 16
MESH = pl.DeviceIdType.MESH
BF16 = jnp.bfloat16
F32 = jnp.float32


def far_first(n):
    return sorted(range(1, n), key=lambda k: (-min(k, n - k), k))


def dot(a, b):
    return jnp.dot(a, b, preferred_element_type=F32)


def dot_nt(a, b):
    return lax.dot_general(a, b, (((1,), (1,)), ((), ())), preferred_element_type=F32)


def dot_tn(a, b):
    return lax.dot_general(a, b, (((0,), (0,)), ((), ())), preferred_element_type=F32)


def kernel(
    n, nb, nb2, slots, scale,
    tab_ref, x_ref, ct_ref, wq_ref, qb_ref, wo_ref, ob_ref,
    lo_ref, ig_ref, dq_ref, dqb_ref, do_ref, dob_ref,
    gat, wos, op, ip, grad, gpf,
    r0, s1, r1, t, r2, v, full, fw, mrg, rcv,
    b0s, b0r, b1s, b1r, b2s, b2r, b3s, b3r, b4s, b4r, b5s, b5r,
    xs, xr, gs, gr_sem,
):
    width = x_ref.shape[1]
    model = width * GROUPS
    qkv = wq_ref.shape[1]
    heads = wo_ref.shape[0]
    qtiles = -(-qkv // LANES)
    otiles = -(-width // LANES)
    orow = qtiles * model
    brow = orow + otiles * GROUPS * heads
    piece_rows = nb * TILE
    part_rows = nb2 * TILE
    score_scale = 1.0 / math.sqrt(HD)

    dp = lax.axis_index("dp")
    grp = lax.axis_index("group")
    c = lax.rem(dp, 2)
    y = lax.rem(lax.div(dp, 2), n)
    z = lax.div(dp, 2 * n)
    other = dp + 1 - 2 * c
    gr = lax.rem(grp + 1, GROUPS)
    gl = lax.rem(grp + 3, GROUPS)
    gx = lax.rem(grp + 2, GROUPS)
    me = (y, z)

    def on_axis(axis, idx):
        return (z * n + idx) * 2 + c if axis == 0 else (idx * n + y) * 2 + c

    def plus(a, k):
        return lax.rem(a + k, n)

    def send(src, dst, ss, rs, d, g):
        return pltpu.make_async_remote_copy(
            src_ref=src, dst_ref=dst, send_sem=ss, recv_sem=rs,
            device_id=(d, g), device_id_type=MESH,
        )

    def rows_of(img):
        return pl.ds(pl.multiple_of(img * IMG, IMG), IMG)

    barrier = pltpu.get_barrier_semaphore()
    pl.semaphore_signal(barrier, inc=1, device_id=(other, grp), device_id_type=MESH)
    for axis in (0, 1):
        for k in range(1, n):
            pl.semaphore_signal(
                barrier, inc=1, device_id=(on_axis(axis, plus(me[axis], k)), grp),
                device_id_type=MESH,
            )
    for g in (gr, gl):
        pl.semaphore_signal(barrier, inc=1, device_id=(dp, g), device_id_type=MESH)

    def stage(img, _):
        rows = rows_of(img)
        gat[0, grp, img] = x_ref[rows]
        row = lax.broadcasted_iota(jnp.int32, (IMG, width), 0)
        keep = row < tab_ref[dp * slots + img, 0]
        gat[1, grp, img] = jnp.where(keep, ct_ref[rows].astype(F32), 0.0).astype(BF16)
        return 0

    lax.fori_loop(0, slots, stage, 0)
    half = IMG // 2
    lo_half = pl.ds(0, half)
    hi_half = pl.ds(half, half)

    def g_copy(arr, img, j):
        ch = arr * slots + img
        ref, dst = (
            (gat.at[arr, grp, img], gr),
            (gat.at[arr, grp, img], gl),
            (gat.at[arr, gl, img, lo_half], gr),
            (gat.at[arr, gr, img, hi_half], gl),
        )[j]
        return send(ref, ref, gs.at[ch, j], gr_sem.at[ch, j], dp, dst)

    def g_in(arr, img, j):
        ch = arr * slots + img
        ref = (
            gat.at[arr, gl, img],
            gat.at[arr, gr, img],
            gat.at[arr, gx, img, lo_half],
            gat.at[arr, gx, img, hi_half],
        )[j]
        return send(ref, ref, gs.at[ch, j], gr_sem.at[ch, j], dp, gr)

    def direct(img):
        for arr in (0, 1):
            for j in (0, 1):
                g_copy(arr, img, j).start()

    def forward(img):
        for arr in (0, 1):
            for j in (0, 1):
                g_in(arr, img, j).wait_recv()
                g_copy(arr, img, j + 2).start()

    pl.semaphore_wait(barrier, 1 + 2 * (n - 1) + 2)
    direct(0)
    direct(1)

    grad[...] = jnp.zeros(grad.shape, F32)
    gpf[...] = jnp.zeros(gpf.shape, F32)
    for s in range(GROUPS):
        wos[s] = wo_ref[:, s * width:(s + 1) * width]
    forward(0)

    def image(img, _):
        @pl.when(img + 2 < slots)
        def _():
            direct(img + 2)

        @pl.when(img + 1 < slots)
        def _():
            forward(img + 1)

        for arr in (0, 1):
            for j in (2, 3):
                g_in(arr, img, j).wait_recv()
        rows = rows_of(img)
        count = tab_ref[dp * slots + img, 0]
        proj = qb_ref[...]
        for s in range(GROUPS):
            proj = proj + dot(gat[0, s, img], wq_ref[s * width:(s + 1) * width, :])
        proj = proj.astype(BF16)
        gmix = dot_nt(gat[1, 0, img], wos[0])
        for s in range(1, GROUPS):
            gmix = gmix + dot_nt(gat[1, s, img], wos[s])
        gmix = gmix.astype(BF16)
        mixed = []
        for h in range(heads // HD):
            at = 3 * HD * h
            q = proj[:, at:at + HD]
            k = proj[:, at + HD:at + 2 * HD]
            val = proj[:, at + 2 * HD:at + 3 * HD]
            gm = gmix[:, h * HD:(h + 1) * HD]
            scores = dot_nt(q, k) * score_scale
            col = lax.broadcasted_iota(jnp.int32, scores.shape, 1)
            scores = jnp.where(col < count, scores, -1e30)
            ex = jnp.exp(scores - jnp.max(scores, axis=-1, keepdims=True))
            probs = ex / jnp.sum(ex, axis=-1, keepdims=True)
            probs_b = probs.astype(BF16)
            mixed.append(dot(probs_b, val).astype(BF16))
            gprobs = dot_nt(gm, val)
            inner = jnp.sum(probs * gprobs, axis=-1, keepdims=True)
            gscores = (probs * (gprobs - inner) * score_scale).astype(BF16)
            gpf[:, at:at + HD] = dot(gscores, k)
            gpf[:, at + HD:at + 2 * HD] = dot_tn(gscores, q)
            gpf[:, at + 2 * HD:at + 3 * HD] = dot_tn(probs_b, gm)
        mixed = jnp.concatenate(mixed, axis=1)
        gproj = gpf[...]
        gsum = jnp.sum(gproj, axis=0, keepdims=True)
        for j in range(qtiles):
            grad[brow + j:brow + j + 1, :] += gsum[:, j * LANES:(j + 1) * LANES]
        osum = jnp.sum(gat[1, grp, img].astype(F32), axis=0, keepdims=True)
        for j in range(otiles):
            w = min(LANES, width - j * LANES)
            at = brow + qtiles + j
            grad[at:at + 1, :w] += osum[:, j * LANES:j * LANES + w]
        gproj_b = gproj.astype(BF16)
        for s in range(GROUPS):
            op[s, rows] = dot(mixed, wos[s]).astype(BF16)
            ip[s, rows] = dot_nt(gproj_b[:, :qkv], wq_ref[s * width:(s + 1) * width, :]).astype(BF16)
            dq = dot_tn(gat[0, s, img], gproj_b)
            for j in range(qtiles):
                at = j * model + s * width
                grad[at:at + width, :] += dq[:, j * LANES:(j + 1) * LANES]
            do = dot_tn(mixed, gat[1, s, img])
            for j in range(otiles):
                w = min(LANES, width - j * LANES)
                at = orow + (j * GROUPS + s) * heads
                grad[at:at + heads, :w] += do[:, j * LANES:j * LANES + w]
        return 0

    lax.fori_loop(0, slots, image, 0)

    order = far_first(n) + [0]

    def piece(cc, s, p):
        return pl.ds(pl.multiple_of(((cc * 2 + s) * n + p) * piece_rows, TILE), piece_rows)

    def l0(s, k):
        p = plus(me[s], k)
        return send(
            grad.at[piece(1 - c, s, p)], r0.at[s, p], b0s.at[s, k], b0r.at[s, k], other, grp
        )

    for k in order:
        for s in (0, 1):
            l0(s, k).start()

    def x_copy(arr, img, j):
        src = (op, ip)[arr]
        ch = arr * slots + img
        lo = pl.ds(pl.multiple_of(img * IMG, half), half)
        hi = pl.ds(pl.multiple_of(img * IMG + half, half), half)
        ref, dst, to = (
            lambda: (src.at[gx, lo], fw.at[ch, 0], gr),
            lambda: (src.at[gx, hi], fw.at[ch, 1], gl),
            lambda: (src.at[gr, hi], rcv.at[ch, 0, 1], gr),
            lambda: (src.at[gl, lo], rcv.at[ch, 1, 0], gl),
            lambda: (mrg.at[ch, 0], rcv.at[ch, 0, 0], gr),
            lambda: (mrg.at[ch, 1], rcv.at[ch, 1, 1], gl),
        )[j]()
        return send(ref, dst, xs.at[ch, j], xr.at[ch, j], dp, to)

    for arr in (0, 1):
        def raw(img, _, arr=arr):
            for j in range(4):
                x_copy(arr, img, j).start()
            return 0
        lax.fori_loop(0, slots, raw, 0)

    def l1(s, k):
        return send(
            s1.at[s, k], r1.at[s, k], b1s.at[s, k], b1r.at[s, k],
            on_axis(s, plus(me[s], k)), grp,
        )

    for k in order:
        for s in (0, 1):
            l0(s, k).wait_recv()
            p = plus(me[s], k)
            total = grad[piece(c, s, p)] + r0[s, p]
            if k:
                s1[s, k] = total.astype(BF16)
                l1(s, k).start()
            else:
                t[s, pl.ds(0, piece_rows)] = total
                rest = part_rows * n - piece_rows
                if rest:
                    t[s, pl.ds(piece_rows, rest)] = jnp.zeros((rest, LANES), F32)

    def merge(arr):
        def step(img, _):
            ch = arr * slots + img
            src = (op, ip)[arr]
            lo = pl.ds(pl.multiple_of(img * IMG, half), half)
            hi = pl.ds(pl.multiple_of(img * IMG + half, half), half)
            x_copy(arr, img, 0).wait_recv()
            mrg[ch, 0] = (src[gr, lo].astype(F32) + fw[ch, 0].astype(F32)).astype(BF16)
            x_copy(arr, img, 4).start()
            x_copy(arr, img, 1).wait_recv()
            mrg[ch, 1] = (src[gl, hi].astype(F32) + fw[ch, 1].astype(F32)).astype(BF16)
            x_copy(arr, img, 5).start()
            return 0
        lax.fori_loop(0, slots, step, 0)

    merge(0)

    def part(q):
        return pl.ds(pl.multiple_of(q * part_rows, TILE), part_rows)

    def l2(s, k):
        q = plus(me[1 - s], k)
        return send(
            t.at[s, part(q)], r2.at[s, k], b2s.at[s, k], b2r.at[s, k], on_axis(1 - s, q), grp,
        )

    near = list(reversed(far_first(n)))
    for s in (0, 1):
        for k in near:
            l1(s, k).wait_recv()
        total = t[s, pl.ds(0, piece_rows)]
        for k in near:
            total = total + r1[s, k].astype(F32)
        t[s, pl.ds(0, piece_rows)] = total
        for k in far_first(n):
            l2(s, k).start()

    merge(1)

    def l3(s, k):
        mine = v.at[s, part(me[1 - s])]
        return send(
            mine, mine, b3s.at[s, k], b3r.at[s, k], on_axis(1 - s, plus(me[1 - s], k)), grp,
        )

    for s in (0, 1):
        for k in near:
            l2(s, k).wait_recv()
        total = t[s, part(me[1 - s])]
        for k in near:
            total = total + r2[s, k]
        v[s, part(me[1 - s])] = (total * scale).astype(BF16)
        for k in far_first(n):
            l3(s, k).start()

    def l4(s, k):
        return send(
            v.at[s, pl.ds(0, piece_rows)], full.at[piece(c, s, me[s])], b4s.at[s, k], b4r.at[s, k],
            on_axis(s, plus(me[s], k)), grp,
        )

    def l5(s, k):
        at = full.at[piece(c, s, plus(me[s], k))]
        return send(at, at, b5s.at[s, k], b5r.at[s, k], other, grp)

    def l3_in(s, k):
        at = v.at[s, part(plus(me[1 - s], n - k))]
        return send(at, at, b3s.at[s, k], b3r.at[s, k], other, grp)

    for s in (0, 1):
        for k in near:
            l3_in(s, k).wait_recv()
        for k in far_first(n):
            l4(s, k).start()
        full[piece(c, s, me[s])] = v[s, pl.ds(0, piece_rows)]
        l5(s, 0).start()

    def l4_in(s, k):
        at = full.at[piece(c, s, plus(me[s], n - k))]
        return send(at, at, b4s.at[s, k], b4r.at[s, k], other, grp)

    for k in near:
        for s in (0, 1):
            l4_in(s, k).wait_recv()
            l5(s, n - k).start()

    def finish(arr):
        def step(img, _):
            ch = arr * slots + img
            for j in range(2, 6):
                x_copy(arr, img, j).wait_recv()
            rows = rows_of(img)
            src = (op, ip)[arr]
            total = src[grp, rows].astype(F32)
            total = total + rcv[ch, 0].reshape(IMG, width).astype(F32)
            total = total + rcv[ch, 1].reshape(IMG, width).astype(F32)
            total = total + gat[arr, grp, img].astype(F32)
            if arr == 0:
                total = total + ob_ref[...]
            row = lax.broadcasted_iota(jnp.int32, total.shape, 0)
            keep = row < tab_ref[dp * slots + img, 0]
            (lo_ref, ig_ref)[arr][rows] = jnp.where(keep, total, 0.0).astype(BF16)
            return 0
        lax.fori_loop(0, slots, step, 0)

    finish(0)
    finish(1)

    def l5_in(s, k):
        at = full.at[piece(1 - c, s, plus(me[s], k))]
        return send(at, at, b5s.at[s, k], b5r.at[s, k], other, grp)

    for k in range(n):
        for s in (0, 1):
            l5_in(s, k).wait_recv()
    for j in range(qtiles):
        w = min(LANES, qkv - j * LANES)
        dq_ref[:, j * LANES:j * LANES + w] = full[j * model:(j + 1) * model, :w]
        dqb_ref[:, j * LANES:j * LANES + w] = full[brow:brow + TILE, :w].astype(F32)[j:j + 1]
    wide = []
    for s in range(GROUPS):
        for j in range(otiles):
            w = min(LANES, width - j * LANES)
            at = orow + (j * GROUPS + s) * heads
            wide.append(full[at:at + heads, :w])
    do_ref[...] = jnp.concatenate(wide, axis=1)
    for j in range(otiles):
        w = min(LANES, width - j * LANES)
        dob_ref[:, j * LANES:j * LANES + w] = (
            full[brow:brow + TILE, :w].astype(F32)[qtiles + j:qtiles + j + 1]
        )
    for k in range(n):
        for s in (0, 1):
            l0(s, k).wait_send()
            l5(s, k).wait_send()
            if k:
                l1(s, k).wait_send()
                l2(s, k).wait_send()
                l3(s, k).wait_send()
                l4(s, k).wait_send()
    for arr in (0, 1):
        def done(img, _, arr=arr):
            for j in range(6):
                x_copy(arr, img, j).wait_send()
            for j in range(4):
                g_copy(arr, img, j).wait_send()
            return 0
        lax.fori_loop(0, slots, done, 0)


def local(tokens, cotangent, slot_table, w_qkv, qkv_bias, w_out, out_bias):
    dp_count = lax.axis_size("dp")
    slots = slot_table.shape[0] // dp_count
    rows, width = tokens.shape
    model, qkv = w_qkv.shape
    heads = w_out.shape[0]
    n = math.isqrt(dp_count // 2)
    scale = 1.0 / math.sqrt(dp_count * slots * IMG)
    used = -(-qkv // LANES) * model // TILE + -(-width // LANES) * GROUPS * heads // TILE + 1
    nb = -(-used // (4 * n))
    nb2 = -(-nb // n)
    piece_rows, part_rows, half = nb * TILE, nb2 * TILE, IMG // 2
    chunks = 2 * slots
    vm = pl.BlockSpec(memory_space=pltpu.VMEM)
    dma = pltpu.SemaphoreType.DMA
    outs = pl.pallas_call(
        functools.partial(kernel, n, nb, nb2, slots, scale),
        out_shape=(
            jax.ShapeDtypeStruct((rows, width), BF16),
            jax.ShapeDtypeStruct((rows, width), BF16),
            jax.ShapeDtypeStruct((model, qkv), BF16),
            jax.ShapeDtypeStruct((1, qkv), F32),
            jax.ShapeDtypeStruct((heads, model), BF16),
            jax.ShapeDtypeStruct((1, width), F32),
        ),
        in_specs=[pl.BlockSpec(memory_space=pltpu.SMEM)] + [vm] * 6,
        out_specs=(vm,) * 6,
        scratch_shapes=[
            pltpu.VMEM((2, GROUPS, slots, IMG, width), BF16),
            pltpu.VMEM((GROUPS, heads, width), BF16),
            pltpu.VMEM((GROUPS, rows, width), BF16),
            pltpu.VMEM((GROUPS, rows, width), BF16),
            pltpu.VMEM((4 * n * piece_rows, LANES), F32),
            pltpu.VMEM((IMG, -(-qkv // LANES) * LANES), F32),
            pltpu.VMEM((2, n, piece_rows, LANES), F32),
            pltpu.VMEM((2, n, piece_rows, LANES), BF16),
            pltpu.VMEM((2, n, piece_rows, LANES), BF16),
            pltpu.VMEM((2, n * part_rows, LANES), F32),
            pltpu.VMEM((2, n, part_rows, LANES), F32),
            pltpu.VMEM((2, n * part_rows, LANES), BF16),
            pltpu.VMEM((4 * n * piece_rows, LANES), BF16),
            pltpu.VMEM((chunks, 2, half, width), BF16),
            pltpu.VMEM((chunks, 2, half, width), BF16),
            pltpu.VMEM((chunks, 2, 2, half, width), BF16),
        ] + [dma((2, n))] * 12 + [dma((chunks, 6))] * 2 + [dma((chunks, 4))] * 2,
        compiler_params=pltpu.CompilerParams(
            collective_id=0, has_side_effects=True, vmem_limit_bytes=50 * 2**20,
        ),
        cost_estimate=pl.CostEstimate(flops=4 * 10**9, bytes_accessed=10**7, transcendentals=0),
    )(slot_table, tokens, cotangent, w_qkv, qkv_bias.reshape(1, qkv), w_out, out_bias.reshape(1, width))
    layer_out, input_grad, dq, dqb, do, dob = outs
    return (layer_out, input_grad, dq, dqb.reshape(qkv), do, dob.reshape(width))


def solution(mesh):
    return jax.shard_map(
        local,
        mesh=mesh,
        in_specs=(
            P("dp", "group"),
            P("dp", "group"),
            P(),
            P(None, "group"),
            P("group"),
            P("group", None),
            P("group"),
        ),
        out_specs=(
            P("dp", "group"),
            P("dp", "group"),
            P(None, "group"),
            P("group"),
            P("group", None),
            P("group"),
        ),
        check_vma=False,
    )
```

time: 217 us -> 117 us (0.54)
  waiting for transfers between devices: 69.9 us -> 0 us
  Pallas kernels: 55.2 us -> 105 us
  local copies, waits for them, and re-layouts: 46.7 us -> 10.4 us
  matrix products: 24.4 us -> 0 us
  between operations: 14.3 us -> 0.7 us
  other arithmetic: 5.61 us -> 0.6 us
    all_gather x2 -> x0, waiting for transfers between devices: 69.2 us -> none  [the longest x1 36.9 us: local(): full_g = lax.all_gather(local_g, 'group', axis=1, tiled=True)]
    pallas_call x1, Pallas kernels: 55.2 us -> 105 us  [local(): pl.pallas_call(functools.partial(kernel, n, nb, nb2, slots, scale), out_s...]
    dot_general x11 -> x0, matrix products: 22.9 us -> none  [the longest x1 3.38 us: local(): projected = jnp.dot(full_x, w_qkv, preferred_element_type=F32) + qkv_bias]
    reshape x5 -> x0, local copies, waits for them, and re-layouts: 13.4 us -> none  [the longest x1 3.96 us: to_blocks(): a.reshape(rows // 16, 16, wide // 128, 128).transpose(0, 2, 1, 3)]
    convert_element_type x4 -> x0, local copies, waits for them, and re-layouts: 7.47 us -> none  [the longest x1 3.52 us: local(): jnp.einsum('rc,dc->rd', grad_proj_b, w_qkv, preferred_element_type=F32)]
    transpose x3 -> x0, local copies, waits for them, and re-layouts: 5.67 us -> none  [the longest x1 3.51 us: to_blocks(): a.reshape(rows // 16, 16, wide // 128, 128).transpose(0, 2, 1, 3)]
    slice x6 -> x0, local copies, waits for them, and re-layouts: 5.1 us -> none  [the longest x1 1.3 us: from_blocks(): full[:na].reshape(rows // 16, wide // 128, 16, 128).transpose(0, 2, 1, 3)]
    concatenate x1 -> x0, other arithmetic: 3.96 us -> none  [to_blocks(): jnp.concatenate([a, b, bias, jnp.zeros((4 * n * nb - used, 16, 128), F32)])]
  transfers between devices with their start and end apart: 2 -> 0, of which waited for: 2 -> 0; matrix products, arithmetic and copies ran while one was open for 1% -> 0% of each run, Pallas kernels for 0% -> 0%
where the time goes in v2:
time: 117 us; the launch traced here: 116 us
  Pallas kernels  105 us (90%)
  local copies, waits for them, and re-layouts  10.4 us (9%)
    pallas_call x1, Pallas kernels, local(): pl.pallas_call(functools.partial(kernel, n, nb, nb2, slots, scale), out_s...  105 us
    unnamed x17, local copies, waits for them, and re-layouts  9.61 us

profile of v2, /device:TPU:1, one launch (start us, length us, event | category | flops | bytes accessed | tf_op | source)
XLA Modules:
  0.0 116.3 jit_solution(7327479948623429433)
XLA Ops:
  0.6 0.0 copy-start.3
  0.6 0.8 reshape.25.ob_ref
  1.4 0.9 copy.13.tab_ref
  2.3 1.3 %copy.14.x_ref = bf16[640,320]{1,0:T(8,128)(2,1)S(1)} copy(bf16[640,320]{0,1:T(8,128)(2,1)} %param.7) | data formatting | bytes 819200 | tf_op args[0]
  3.6 1.3 %copy.15.ct_ref = bf16[640,320]{1,0:T(8,128)(2,1)S(1)} copy(bf16[640,320]{0,1:T(8,128)(2,1)} %param.8) | data formatting | bytes 819200 | tf_op args[1]
  4.8 0.0 copy-done.3
  4.8 0.0 copy-start
  4.9 0.0 copy-start.1
  4.9 1.5 %copy.16.wq_ref = bf16[1280,480]{1,0:T(8,128)(2,1)} copy(bf16[1280,480]{0,1:T(8,128)(2,1)S(1)} %copy-done.3) | data formatting | bytes 2457600 | tf_op args[3]
  6.3 0.0 copy-done
  6.3 0.0 copy-done.1
  6.3 104.6 %shard_map.118 = (bf16[640,320]{1,0:T(8,128)(2,1)S(1)}, bf16[640,320]{1,0:T(8,128)(2,1)S(1)}, bf16[1280,480]{1,0:T(8,128)(2,1)}, f32[1,480]{1,0:T(1,128)S(1)}, b...) custom-call(s32[640,2]{1,0:T(8,128)S(1)} %copy.13.tab_ref, bf16[640,320]{1,0:T(8,128)(2,1)S(1)} %copy.14.x_ref, ...), custom_call_target="tpu_custom_call" | custom-call | flops 4000000000 | bytes 10000000 | tf_op jit(solution)/shard_map/pallas_call | solution.py:440
  110.9 0.0 copy-start.2
  111.0 1.0 copy.17
  111.9 0.6 reduce
  112.5 1.0 copy.18
  113.5 0.0 copy-done.2
  113.5 1.5 %copy.19 = bf16[1280,480]{0,1:T(8,128)(2,1)} copy(bf16[1280,480]{1,0:T(8,128)(2,1)S(1)} %copy-done.2) | data formatting | bytes 2457600
  114.9 0.6 copy.22
  115.5 0.8 copy.23
Async XLA Ops:
  0.6 4.2 %copy-start.3 = (bf16[1280,480]{0,1:T(8,128)(2,1)S(1)}, bf16[1280,480]{0,1:T(8,128)(2,1)}, u32[]{:S(2)}) copy-start(bf16[1280,480]{0,1:T(8,128)(2,1)} %param.10) | copy-start | bytes 3686404
  4.8 1.5 %copy-start = (bf16[160,1280]{1,0:T(8,128)(2,1)S(1)}, bf16[160,1280]{1,0:T(8,128)(2,1)}, u32[]{:S(2)}) copy-start(bf16[160,1280]{1,0:T(8,128)(2,1)} %wo_ref.1) | copy-start | bytes 1228804
  4.9 1.5 %copy-start.1 = (f32[480]{0:T(512)S(1)}, f32[480]{0:T(512)}, u32[]{:S(2)}) copy-start(f32[480]{0:T(512)} %param.11) | copy-start | bytes 5764
  110.9 2.5 %copy-start.2 = (bf16[1280,480]{1,0:T(8,128)(2,1)S(1)}, bf16[1280,480]{1,0:T(8,128)(2,1)}, u32[]{:S(2)}) copy-start(bf16[1280,480]{1,0:T(8,128)(2,1)} %get-tuple-element.20) | copy-start | bytes 3686404

commit v3 on v2

v3 whole, which is shorter than its diff:
```python
import functools
import math

import jax
import jax.numpy as jnp
from jax import lax
from jax.experimental import pallas as pl
from jax.experimental.pallas import tpu as pltpu
from jax.sharding import PartitionSpec as P

HD = 80
IMG = 128
GROUPS = 4
LANES = 128
TILE = 16
MESH = pl.DeviceIdType.MESH
BF16 = jnp.bfloat16
F32 = jnp.float32


def far_first(n):
    return sorted(range(1, n), key=lambda k: (-min(k, n - k), k))


def dot(a, b):
    return jnp.dot(a, b, preferred_element_type=F32)


def dot_nt(a, b):
    return lax.dot_general(a, b, (((1,), (1,)), ((), ())), preferred_element_type=F32)


def dot_tn(a, b):
    return lax.dot_general(a, b, (((0,), (0,)), ((), ())), preferred_element_type=F32)


def kernel(
    n, nb, nb2, slots, scale,
    tab_ref, x_ref, ct_ref, wq_ref, qb_ref, wo_ref, ob_ref,
    lo_ref, ig_ref, dq_ref, dqb_ref, do_ref, dob_ref,
    gat, ctv, wq, wqn, wo, won, qbb, obb, op, ip, grad, gpf, qsum, osum, gps, mixs,
    r0, s1, r1, t, r2, v, full, fw, mrg, rcv,
    b0s, b0r, b1s, b1r, b2s, b2r, b3s, b3r, b4s, b4r, b5s, b5r,
    xs, xr, gs, gr_sem, ls,
):
    width = x_ref.shape[0]
    model = width * GROUPS
    qkv = wq_ref.shape[0]
    heads = wo_ref.shape[0]
    both = qkv + heads
    tiles = model // LANES
    qtiles = -(-qkv // LANES)
    otiles = -(-width // LANES)
    brow = tiles * both
    piece_rows = nb * TILE
    part_rows = nb2 * TILE
    score_scale = 1.0 / math.sqrt(HD)

    dp = lax.axis_index("dp")
    grp = lax.axis_index("group")
    c = lax.rem(dp, 2)
    y = lax.rem(lax.div(dp, 2), n)
    z = lax.div(dp, 2 * n)
    other = dp + 1 - 2 * c
    gr = lax.rem(grp + 1, GROUPS)
    gl = lax.rem(grp + 3, GROUPS)
    gx = lax.rem(grp + 2, GROUPS)
    me = (y, z)

    def on_axis(axis, idx):
        return (z * n + idx) * 2 + c if axis == 0 else (idx * n + y) * 2 + c

    def plus(a, k):
        return lax.rem(a + k, n)

    def send(src, dst, ss, rs, d, g):
        return pltpu.make_async_remote_copy(
            src_ref=src, dst_ref=dst, send_sem=ss, recv_sem=rs,
            device_id=(d, g), device_id_type=MESH,
        )

    half = width // 2

    def shard(g):
        return pl.ds(pl.multiple_of(g * width, TILE), width)

    def lo_of(g):
        return pl.ds(pl.multiple_of(g * width, TILE), half)

    def hi_of(g):
        return pl.ds(pl.multiple_of(g * width + half, TILE), half)

    barrier = pltpu.get_barrier_semaphore()
    pl.semaphore_signal(barrier, inc=1, device_id=(other, grp), device_id_type=MESH)
    for axis in (0, 1):
        for k in range(1, n):
            pl.semaphore_signal(
                barrier, inc=1, device_id=(on_axis(axis, plus(me[axis], k)), grp),
                device_id_type=MESH,
            )
    for g in (gr, gl):
        pl.semaphore_signal(barrier, inc=1, device_id=(dp, g), device_id_type=MESH)

    loads = [
        pltpu.make_async_copy(
            x_ref.at[:, i * IMG:(i + 1) * IMG], gat.at[0, i, shard(grp)], ls.at[i]
        )
        for i in range(slots)
    ]
    load_ct = pltpu.make_async_copy(ct_ref, ctv, ls.at[slots])
    load_wq = pltpu.make_async_copy(wq_ref, wq, ls.at[slots + 1])
    load_wo = pltpu.make_async_copy(wo_ref, wo, ls.at[slots + 2])
    load_ct.start()
    for cp in loads:
        cp.start()
    load_wq.start()
    load_wo.start()

    def lanes_below(img, shape):
        lane = lax.broadcasted_iota(jnp.int32, shape, 1)
        return lane < tab_ref[0, dp * slots + img]

    load_ct.wait()
    for i in range(slots):
        rows = ctv[:, i * IMG:(i + 1) * IMG].astype(F32)
        gat[1, i, shard(grp)] = jnp.where(lanes_below(i, rows.shape), rows, 0.0).astype(BF16)
    for cp in loads:
        cp.wait()

    def g_copy(arr, img, j):
        ch = arr * slots + img
        at, to = (
            lambda: (shard(grp), gr),
            lambda: (shard(grp), gl),
            lambda: (lo_of(gl), gr),
            lambda: (hi_of(gr), gl),
        )[j]()
        ref = gat.at[arr, img, at]
        return send(ref, ref, gs.at[ch, j], gr_sem.at[ch, j], dp, to)

    def g_in(arr, img, j):
        ch = arr * slots + img
        at = (lambda: shard(gl), lambda: shard(gr), lambda: lo_of(gx), lambda: hi_of(gx))[j]()
        ref = gat.at[arr, img, at]
        return send(ref, ref, gs.at[ch, j], gr_sem.at[ch, j], dp, gr)

    def direct(img):
        for arr in (0, 1):
            for j in (0, 1):
                g_copy(arr, img, j).start()

    def forward(img):
        for arr in (0, 1):
            for j in (0, 1):
                g_in(arr, img, j).wait_recv()
                g_copy(arr, img, j + 2).start()

    pl.semaphore_wait(barrier, 1 + 2 * (n - 1) + 2)
    direct(0)
    direct(1)

    grad[...] = jnp.zeros(grad.shape, F32)
    qsum[...] = jnp.zeros(qsum.shape, F32)
    osum[...] = jnp.zeros(osum.shape, F32)
    qbb[...] = jnp.broadcast_to(qb_ref[...].reshape(1, qkv), (IMG, qkv)).T
    obb[...] = jnp.broadcast_to(ob_ref[...].reshape(1, width), (IMG, width)).T
    load_wq.wait()
    load_wo.wait()
    for j in range(tiles):
        wqn[j * LANES:(j + 1) * LANES] = wq[:, j * LANES:(j + 1) * LANES].T
        won[j * LANES:(j + 1) * LANES] = wo[:, j * LANES:(j + 1) * LANES].T
    forward(0)

    def image_grads(img):
        proj = (dot(wq[...], gat[0, img]) + qbb[...]).astype(BF16)
        gmix = dot(wo[...], gat[1, img]).astype(BF16)
        for h in range(heads // HD):
            at = 3 * HD * h
            q = proj[at:at + HD]
            k = proj[at + HD:at + 2 * HD]
            val = proj[at + 2 * HD:at + 3 * HD]
            gm = gmix[h * HD:(h + 1) * HD]
            scores = dot_tn(k, q) * score_scale
            row = lax.broadcasted_iota(jnp.int32, scores.shape, 0)
            scores = jnp.where(row < tab_ref[0, dp * slots + img], scores, -1e30)
            ex = jnp.exp(scores - jnp.max(scores, axis=0, keepdims=True))
            probs = ex / jnp.sum(ex, axis=0, keepdims=True)
            probs_b = probs.astype(BF16)
            mixs[h * HD:(h + 1) * HD] = dot(val, probs_b).astype(BF16)
            gprobs = dot_tn(val, gm)
            inner = jnp.sum(probs * gprobs, axis=0, keepdims=True)
            gscores = (probs * (gprobs - inner) * score_scale).astype(BF16)
            gpf[at:at + HD] = dot(k, gscores)
            gpf[at + HD:at + 2 * HD] = dot_nt(q, gscores)
            gpf[at + 2 * HD:at + 3 * HD] = dot_nt(gm, probs_b)
        gproj = gpf[...]
        qsum[...] += gproj
        osum[...] += gat[1, img, shard(grp)].astype(F32)
        gps[...] = gproj.astype(BF16)
        step = 2 * LANES
        for j in range(0, model, step):
            dq = dot_nt(gps[...], gat[0, img, j:j + step])
            do = dot_nt(mixs[...], gat[1, img, j:j + step])
            for i in range(0, step, LANES):
                at = (j + i) // LANES * both
                grad[at:at + qkv] += dq[:, i:i + LANES]
                grad[at + qkv:at + both] += do[:, i:i + LANES]

    def image_parts(img):
        op[img] = dot(won[...], mixs[...]).astype(BF16)
        ip[img] = dot(wqn[...], gps[...]).astype(BF16)

    def image(img, _):
        @pl.when(img + 2 < slots)
        def _():
            direct(img + 2)

        @pl.when(img + 1 < slots)
        def _():
            forward(img + 1)

        for arr in (0, 1):
            for j in (2, 3):
                g_in(arr, img, j).wait_recv()
        image_grads(img)

        @pl.when(img + 1 < slots)
        def _():
            image_parts(img)

        return 0

    lax.fori_loop(0, slots, image, 0)
    qtot = jnp.sum(qsum[...].T, axis=0, keepdims=True)
    otot = jnp.sum(osum[...].T, axis=0, keepdims=True)
    for j in range(qtiles):
        w = min(LANES, qkv - j * LANES)
        grad[brow + j:brow + j + 1, :w] = qtot[:, j * LANES:j * LANES + w]
    for j in range(otiles):
        w = min(LANES, width - j * LANES)
        at = brow + qtiles + j
        grad[at:at + 1, :w] = otot[:, j * LANES:j * LANES + w]

    order = far_first(n) + [0]

    def piece(cc, s, p):
        return pl.ds(pl.multiple_of(((cc * 2 + s) * n + p) * piece_rows, TILE), piece_rows)

    def l0(s, k):
        p = plus(me[s], k)
        return send(
            grad.at[piece(1 - c, s, p)], r0.at[s, p], b0s.at[s, k], b0r.at[s, k], other, grp
        )

    for k in order:
        for s in (0, 1):
            l0(s, k).start()
    image_parts(slots - 1)

    def x_copy(arr, img, j):
        src = (op, ip)[arr]
        ch = arr * slots + img
        ref, dst, to = (
            lambda: (src.at[img, lo_of(gx)], fw.at[ch, 0], gr),
            lambda: (src.at[img, hi_of(gx)], fw.at[ch, 1], gl),
            lambda: (src.at[img, hi_of(gr)], rcv.at[ch, 0, 1], gr),
            lambda: (src.at[img, lo_of(gl)], rcv.at[ch, 1, 0], gl),
            lambda: (mrg.at[ch, 0], rcv.at[ch, 0, 0], gr),
            lambda: (mrg.at[ch, 1], rcv.at[ch, 1, 1], gl),
        )[j]()
        return send(ref, dst, xs.at[ch, j], xr.at[ch, j], dp, to)

    for arr in (0, 1):
        def raw(img, _, arr=arr):
            for j in range(4):
                x_copy(arr, img, j).start()
            return 0
        lax.fori_loop(0, slots, raw, 0)

    def l1(s, k):
        return send(
            s1.at[s, k], r1.at[s, k], b1s.at[s, k], b1r.at[s, k],
            on_axis(s, plus(me[s], k)), grp,
        )

    for k in order:
        for s in (0, 1):
            l0(s, k).wait_recv()
            p = plus(me[s], k)
            total = grad[piece(c, s, p)] + r0[s, p]
            if k:
                s1[s, k] = total.astype(BF16)
                l1(s, k).start()
            else:
                t[s, pl.ds(0, piece_rows)] = total
                rest = part_rows * n - piece_rows
                if rest:
                    t[s, pl.ds(piece_rows, rest)] = jnp.zeros((rest, LANES), F32)

    def merge(arr):
        def step(img, _):
            ch = arr * slots + img
            src = (op, ip)[arr]
            x_copy(arr, img, 0).wait_recv()
            mrg[ch, 0] = (src[img, lo_of(gr)].astype(F32) + fw[ch, 0].astype(F32)).astype(BF16)
            x_copy(arr, img, 4).start()
            x_copy(arr, img, 1).wait_recv()
            mrg[ch, 1] = (src[img, hi_of(gl)].astype(F32) + fw[ch, 1].astype(F32)).astype(BF16)
            x_copy(arr, img, 5).start()
            return 0
        lax.fori_loop(0, slots, step, 0)

    merge(0)

    def part(q):
        return pl.ds(pl.multiple_of(q * part_rows, TILE), part_rows)

    def l2(s, k):
        q = plus(me[1 - s], k)
        return send(
            t.at[s, part(q)], r2.at[s, k], b2s.at[s, k], b2r.at[s, k], on_axis(1 - s, q), grp,
        )

    near = list(reversed(far_first(n)))
    for s in (0, 1):
        for k in near:
            l1(s, k).wait_recv()
        total = t[s, pl.ds(0, piece_rows)]
        for k in near:
            total = total + r1[s, k].astype(F32)
        t[s, pl.ds(0, piece_rows)] = total
        for k in far_first(n):
            l2(s, k).start()

    merge(1)

    def l3(s, k):
        mine = v.at[s, part(me[1 - s])]
        return send(
            mine, mine, b3s.at[s, k], b3r.at[s, k], on_axis(1 - s, plus(me[1 - s], k)), grp,
        )

    for s in (0, 1):
        for k in near:
            l2(s, k).wait_recv()
        total = t[s, part(me[1 - s])]
        for k in near:
            total = total + r2[s, k]
        v[s, part(me[1 - s])] = (total * scale).astype(BF16)
        for k in far_first(n):
            l3(s, k).start()

    def l4(s, k):
        return send(
            v.at[s, pl.ds(0, piece_rows)], full.at[piece(c, s, me[s])], b4s.at[s, k], b4r.at[s, k],
            on_axis(s, plus(me[s], k)), grp,
        )

    def l5(s, k):
        at = full.at[piece(c, s, plus(me[s], k))]
        return send(at, at, b5s.at[s, k], b5r.at[s, k], other, grp)

    def l3_in(s, k):
        at = v.at[s, part(plus(me[1 - s], n - k))]
        return send(at, at, b3s.at[s, k], b3r.at[s, k], other, grp)

    for s in (0, 1):
        for k in near:
            l3_in(s, k).wait_recv()
        for k in far_first(n):
            l4(s, k).start()
        full[piece(c, s, me[s])] = v[s, pl.ds(0, piece_rows)]
        l5(s, 0).start()

    def l4_in(s, k):
        at = full.at[piece(c, s, plus(me[s], n - k))]
        return send(at, at, b4s.at[s, k], b4r.at[s, k], other, grp)

    for k in near:
        for s in (0, 1):
            l4_in(s, k).wait_recv()
            l5(s, n - k).start()

    def finish(arr):
        def step(img, _):
            ch = arr * slots + img
            for j in range(2, 6):
                x_copy(arr, img, j).wait_recv()
            src = (op, ip)[arr]
            total = src[img, shard(grp)].astype(F32)
            total = total + rcv[ch, 0].reshape(width, IMG).astype(F32)
            total = total + rcv[ch, 1].reshape(width, IMG).astype(F32)
            total = total + gat[arr, img, shard(grp)].astype(F32)
            if arr == 0:
                total = total + obb[...]
            total = jnp.where(lanes_below(img, total.shape), total, 0.0).astype(BF16)
            (lo_ref, ig_ref)[arr][:, pl.ds(pl.multiple_of(img * IMG, IMG), IMG)] = total
            return 0
        lax.fori_loop(0, slots, step, 0)

    finish(0)
    finish(1)

    def l5_in(s, k):
        at = full.at[piece(1 - c, s, plus(me[s], k))]
        return send(at, at, b5s.at[s, k], b5r.at[s, k], other, grp)

    for k in range(n):
        for s in (0, 1):
            l5_in(s, k).wait_recv()
    for j in range(tiles):
        at = j * both
        dq_ref[:, j * LANES:(j + 1) * LANES] = full[at:at + qkv]
        do_ref[:, j * LANES:(j + 1) * LANES] = full[at + qkv:at + both]
    sums = full[brow:brow + TILE].astype(F32)
    for ref, size, first in ((dqb_ref, qkv, 0), (dob_ref, width, qtiles)):
        for j in range(-(-size // LANES)):
            w = min(LANES, size - j * LANES)
            ref[:, j * LANES:j * LANES + w] = sums[first + j:first + j + 1, :w]
    for k in range(n):
        for s in (0, 1):
            l0(s, k).wait_send()
            l5(s, k).wait_send()
            if k:
                l1(s, k).wait_send()
                l2(s, k).wait_send()
                l3(s, k).wait_send()
                l4(s, k).wait_send()
    for arr in (0, 1):
        def done(img, _, arr=arr):
            for j in range(6):
                x_copy(arr, img, j).wait_send()
            for j in range(4):
                g_copy(arr, img, j).wait_send()
            return 0
        lax.fori_loop(0, slots, done, 0)


def local(tokens, cotangent, slot_table, w_qkv, qkv_bias, w_out, out_bias):
    dp_count = lax.axis_size("dp")
    slots = slot_table.shape[0] // dp_count
    rows, width = tokens.shape
    model, qkv = w_qkv.shape
    heads = w_out.shape[0]
    n = math.isqrt(dp_count // 2)
    scale = 1.0 / math.sqrt(dp_count * slots * IMG)
    used = (qkv + heads) // TILE * (model // LANES) + 1
    nb = -(-used // (4 * n))
    nb2 = -(-nb // n)
    piece_rows, part_rows, half = nb * TILE, nb2 * TILE, width // 2
    chunks = 2 * slots
    vm = pl.BlockSpec(memory_space=pltpu.VMEM)
    hbm = pl.BlockSpec(memory_space=pl.ANY)
    smem = pl.BlockSpec(memory_space=pltpu.SMEM)
    dma = pltpu.SemaphoreType.DMA
    outs = pl.pallas_call(
        functools.partial(kernel, n, nb, nb2, slots, scale),
        out_shape=(
            jax.ShapeDtypeStruct((width, rows), BF16),
            jax.ShapeDtypeStruct((width, rows), BF16),
            jax.ShapeDtypeStruct((qkv, model), BF16),
            jax.ShapeDtypeStruct((1, qkv), F32),
            jax.ShapeDtypeStruct((heads, model), BF16),
            jax.ShapeDtypeStruct((1, width), F32),
        ),
        in_specs=[smem, hbm, hbm, hbm, vm, hbm, vm],
        out_specs=(vm,) * 6,
        scratch_shapes=[
            pltpu.VMEM((2, slots, model, IMG), BF16),
            pltpu.VMEM((width, rows), BF16),
            pltpu.VMEM((qkv, model), BF16),
            pltpu.VMEM((model, qkv), BF16),
            pltpu.VMEM((heads, model), BF16),
            pltpu.VMEM((model, heads), BF16),
            pltpu.VMEM((qkv, IMG), F32),
            pltpu.VMEM((width, IMG), F32),
            pltpu.VMEM((slots, model, IMG), BF16),
            pltpu.VMEM((slots, model, IMG), BF16),
            pltpu.VMEM((4 * n * piece_rows, LANES), F32),
            pltpu.VMEM((qkv, IMG), F32),
            pltpu.VMEM((qkv, IMG), F32),
            pltpu.VMEM((width, IMG), F32),
            pltpu.VMEM((qkv, IMG), BF16),
            pltpu.VMEM((heads, IMG), BF16),
            pltpu.VMEM((2, n, piece_rows, LANES), F32),
            pltpu.VMEM((2, n, piece_rows, LANES), BF16),
            pltpu.VMEM((2, n, piece_rows, LANES), BF16),
            pltpu.VMEM((2, n * part_rows, LANES), F32),
            pltpu.VMEM((2, n, part_rows, LANES), F32),
            pltpu.VMEM((2, n * part_rows, LANES), BF16),
            pltpu.VMEM((4 * n * piece_rows, LANES), BF16),
            pltpu.VMEM((chunks, 2, half, IMG), BF16),
            pltpu.VMEM((chunks, 2, half, IMG), BF16),
            pltpu.VMEM((chunks, 2, 2, half, IMG), BF16),
        ] + [dma((2, n))] * 12 + [dma((chunks, 6))] * 2 + [dma((chunks, 4))] * 2 + [dma((slots + 3,))],
        compiler_params=pltpu.CompilerParams(
            collective_id=0, has_side_effects=True, vmem_limit_bytes=50 * 2**20,
        ),
        cost_estimate=pl.CostEstimate(flops=4 * 10**9, bytes_accessed=10**7, transcendentals=0),
    )(slot_table.T, tokens.T, cotangent.T, w_qkv.T, qkv_bias.reshape(1, qkv), w_out, out_bias.reshape(1, width))
    layer_out, input_grad, dq, dqb, do, dob = outs
    return (layer_out.T, input_grad.T, dq.T, dqb.reshape(qkv), do, dob.reshape(width))


def solution(mesh):
    return jax.shard_map(
        local,
        mesh=mesh,
        in_specs=(
            P("dp", "group"),
            P("dp", "group"),
            P(),
            P(None, "group"),
            P("group"),
            P("group", None),
            P("group"),
        ),
        out_specs=(
            P("dp", "group"),
            P("dp", "group"),
            P(None, "group"),
            P("group"),
            P("group", None),
            P("group"),
        ),
        check_vma=False,
    )
```

time: 117 us -> 99.5 us (0.85)
  Pallas kernels: 105 us -> 89 us
  local copies, waits for them, and re-layouts: 10.4 us -> 8.92 us
    pallas_call x1, Pallas kernels: 105 us -> 89 us  [local(): pl.pallas_call(functools.partial(kernel, n, nb, nb2, slots, scale), out_s...]
    unnamed x17 -> x15, local copies, waits for them, and re-layouts: 9.61 us -> 8.23 us
where the time goes in v3:
time: 99.5 us; the launch traced here: 99.1 us
  Pallas kernels  89 us (89%)
  local copies, waits for them, and re-layouts  8.92 us (9%)
    pallas_call x1, Pallas kernels, local(): pl.pallas_call(functools.partial(kernel, n, nb, nb2, slots, scale), out_s...  89 us
    unnamed x15, local copies, waits for them, and re-layouts  8.23 us

profile of v3, /device:TPU:1, one launch (start us, length us, event | category | flops | bytes accessed | tf_op | source)
XLA Modules:
  0.0 99.1 jit_solution(14690304276747429181)
XLA Ops:
  0.6 0.7 reshape.25.ob_ref
  1.3 0.0 copy-start
  1.3 1.0 %copy-done = bf16[640,320]{0,1:T(8,128)(2,1)S(1)} copy-done((bf16[640,320]{0,1:T(8,128)(2,1)S(1)}, bf16[640,320]{0,1:T(8,128)(2,1)}, u32[]{:S(2)}) %copy-start) | copy-done | bytes 409624
  2.3 0.0 copy-start.1
  2.3 1.0 %copy-done.1 = bf16[640,320]{0,1:T(8,128)(2,1)S(1)} copy-done((bf16[640,320]{0,1:T(8,128)(2,1)S(1)}, bf16[640,320]{0,1:T(8,128)(2,1)}, u32[]{:S(2)}) %copy-start.1) | copy-done | bytes 409624
  3.3 0.0 copy-start.2
  3.3 1.0 %copy-done.2 = bf16[160,1280]{1,0:T(8,128)(2,1)S(1)} copy-done((bf16[160,1280]{1,0:T(8,128)(2,1)S(1)}, bf16[160,1280]{1,0:T(8,128)(2,1)}, u32[]{:S(2)}) %copy-start.2) | copy-done | bytes 409624
  4.3 0.0 copy-start.3
  4.3 0.7 copy-done.3
  5.0 0.0 copy-start.4
  5.0 0.7 copy-done.4
  5.7 89.0 %shard_map.118 = (bf16[320,640]{1,0:T(8,128)(2,1)S(1)}, bf16[320,640]{1,0:T(8,128)(2,1)S(1)}, bf16[480,1280]{1,0:T(8,128)(2,1)S(1)}, f32[1,480]{1,0:T(1,128)S(1)...) custom-call(s32[2,640]{1,0:T(2,128)S(1)} %bitcast.15, bf16[320,640]{1,0:T(8,128)(2,1)S(1)} %bitcast.13, ...), custom_call_target="tpu_custom_call" | custom-call | flops 4000000000 | bytes 10000000 | tf_op jit(solution)/shard_map/pallas_call | solution.py:456
  94.7 0.6 reduce
  95.3 0.8 copy.18
  96.0 0.8 copy.19
  96.8 1.0 %copy.20 = bf16[1280,480]{0,1:T(8,128)(2,1)} copy(bf16[1280,480]{0,1:T(8,128)(2,1)S(1)} %bitcast.9) | data formatting | bytes 2457600
  97.8 0.6 copy.21
  98.4 0.8 copy.22
Async XLA Ops:
  1.3 1.0 %copy-start = (bf16[640,320]{0,1:T(8,128)(2,1)S(1)}, bf16[640,320]{0,1:T(8,128)(2,1)}, u32[]{:S(2)}) copy-start(bf16[640,320]{0,1:T(8,128)(2,1)} %param.7) | copy-start | bytes 1228804
  2.3 1.0 %copy-start.1 = (bf16[640,320]{0,1:T(8,128)(2,1)S(1)}, bf16[640,320]{0,1:T(8,128)(2,1)}, u32[]{:S(2)}) copy-start(bf16[640,320]{0,1:T(8,128)(2,1)} %param.8) | copy-start | bytes 1228804
  3.3 1.0 %copy-start.2 = (bf16[160,1280]{1,0:T(8,128)(2,1)S(1)}, bf16[160,1280]{1,0:T(8,128)(2,1)}, u32[]{:S(2)}) copy-start(bf16[160,1280]{1,0:T(8,128)(2,1)} %wo_ref.1) | copy-start | bytes 1228804
  4.3 0.7 copy-start.3
  5.0 0.7 copy-start.4

commit v4 on v3

--- a/solution.py
+++ b/solution.py
@@ -38,8 +38,8 @@
     n, nb, nb2, slots, scale,
     tab_ref, x_ref, ct_ref, wq_ref, qb_ref, wo_ref, ob_ref,
     lo_ref, ig_ref, dq_ref, dqb_ref, do_ref, dob_ref,
-    gat, ctv, wq, wqn, wo, won, qbb, obb, op, ip, grad, gpf, qsum, osum, gps, mixs,
-    r0, s1, r1, t, r2, v, full, fw, mrg, rcv,
+    gat, ctv, tab, wq, wqn, wo, won, qb, ob, qbb, obb, op, ip, grad, gpf, qsum, osum, gps, mixs,
+    r0, s1, r1, m1, t, r2, v, full, fw, mrg, rcv,
     b0s, b0r, b1s, b1r, b2s, b2r, b3s, b3r, b4s, b4r, b5s, b5r,
     xs, xr, gs, gr_sem, ls,
 ):
@@ -110,16 +110,23 @@
     load_ct = pltpu.make_async_copy(ct_ref, ctv, ls.at[slots])
     load_wq = pltpu.make_async_copy(wq_ref, wq, ls.at[slots + 1])
     load_wo = pltpu.make_async_copy(wo_ref, wo, ls.at[slots + 2])
+    load_tab = pltpu.make_async_copy(tab_ref, tab, ls.at[slots + 3])
+    load_qb = pltpu.make_async_copy(qb_ref, qb, ls.at[slots + 4])
+    load_ob = pltpu.make_async_copy(ob_ref, ob, ls.at[slots + 5])
+    load_tab.start()
     load_ct.start()
     for cp in loads:
         cp.start()
     load_wq.start()
     load_wo.start()
+    load_qb.start()
+    load_ob.start()
 
     def lanes_below(img, shape):
         lane = lax.broadcasted_iota(jnp.int32, shape, 1)
-        return lane < tab_ref[0, dp * slots + img]
-
+        return lane < tab[0, dp * slots + img]
+
+    load_tab.wait()
     load_ct.wait()
     for i in range(slots):
         rows = ctv[:, i * IMG:(i + 1) * IMG].astype(F32)
@@ -162,10 +169,12 @@
     grad[...] = jnp.zeros(grad.shape, F32)
     qsum[...] = jnp.zeros(qsum.shape, F32)
     osum[...] = jnp.zeros(osum.shape, F32)
-    qbb[...] = jnp.broadcast_to(qb_ref[...].reshape(1, qkv), (IMG, qkv)).T
-    obb[...] = jnp.broadcast_to(ob_ref[...].reshape(1, width), (IMG, width)).T
+    load_qb.wait()
+    load_ob.wait()
     load_wq.wait()
     load_wo.wait()
+    qbb[...] = jnp.broadcast_to(qb[...].reshape(1, qkv), (IMG, qkv)).T
+    obb[...] = jnp.broadcast_to(ob[...].reshape(1, width), (IMG, width)).T
     for j in range(tiles):
         wqn[j * LANES:(j + 1) * LANES] = wq[:, j * LANES:(j + 1) * LANES].T
         won[j * LANES:(j + 1) * LANES] = wo[:, j * LANES:(j + 1) * LANES].T
@@ -182,7 +191,7 @@
             gm = gmix[h * HD:(h + 1) * HD]
             scores = dot_tn(k, q) * score_scale
             row = lax.broadcasted_iota(jnp.int32, scores.shape, 0)
-            scores = jnp.where(row < tab_ref[0, dp * slots + img], scores, -1e30)
+            scores = jnp.where(row < tab[0, dp * slots + img], scores, -1e30)
             ex = jnp.exp(scores - jnp.max(scores, axis=0, keepdims=True))
             probs = ex / jnp.sum(ex, axis=0, keepdims=True)
             probs_b = probs.astype(BF16)
@@ -277,20 +286,34 @@
             return 0
         lax.fori_loop(0, slots, raw, 0)
 
+    tree = n == 8
+    cut = nb // 2 * TILE
+    head_rows, tail_rows = pl.ds(0, cut), pl.ds(cut, piece_rows - cut)
+
     def l1(s, k):
-        return send(
-            s1.at[s, k], r1.at[s, k], b1s.at[s, k], b1r.at[s, k],
-            on_axis(s, plus(me[s], k)), grp,
-        )
+        ref, dst, to = s1.at[s, k], r1.at[s, k], k
+        if tree and k == 3:
+            to = 1
+        elif tree and k == 5:
+            to = 7
+        elif tree and k == 4:
+            ref, dst, to = s1.at[s, 4, head_rows], r1.at[s, 4, head_rows], 2
+        elif tree and k == 0:
+            ref, dst, to = s1.at[s, 4, tail_rows], r1.at[s, 4, tail_rows], 6
+        return send(ref, dst, b1s.at[s, k], b1r.at[s, k], on_axis(s, plus(me[s], to)), grp)
 
     for k in order:
         for s in (0, 1):
             l0(s, k).wait_recv()
             p = plus(me[s], k)
             total = grad[piece(c, s, p)] + r0[s, p]
-            if k:
+            if tree and k in (2, 6):
+                m1[s, k // 4] = total
+            elif k:
                 s1[s, k] = total.astype(BF16)
                 l1(s, k).start()
+                if tree and k == 4:
+                    l1(s, 0).start()
             else:
                 t[s, pl.ds(0, piece_rows)] = total
                 rest = part_rows * n - piece_rows
@@ -310,6 +333,23 @@
             return 0
         lax.fori_loop(0, slots, step, 0)
 
+    if tree:
+        for s in (0, 1):
+            l1(s, 3).wait_recv()
+            l1(s, 4).wait_recv()
+            s1[s, 2, head_rows] = (
+                m1[s, 0, head_rows] + r1[s, 3, head_rows].astype(F32) + r1[s, 4, head_rows].astype(F32)
+            ).astype(BF16)
+            s1[s, 2, tail_rows] = (m1[s, 0, tail_rows] + r1[s, 3, tail_rows].astype(F32)).astype(BF16)
+            l1(s, 2).start()
+            l1(s, 5).wait_recv()
+            l1(s, 0).wait_recv()
+            s1[s, 6, head_rows] = (m1[s, 1, head_rows] + r1[s, 5, head_rows].astype(F32)).astype(BF16)
+            s1[s, 6, tail_rows] = (
+                m1[s, 1, tail_rows] + r1[s, 5, tail_rows].astype(F32) + r1[s, 4, tail_rows].astype(F32)
+            ).astype(BF16)
+            l1(s, 6).start()
+
     merge(0)
 
     def part(q):
@@ -322,17 +362,16 @@
         )
 
     near = list(reversed(far_first(n)))
+    last = [1, 7, 2, 6] if tree else near
     for s in (0, 1):
-        for k in near:
+        for k in last:
             l1(s, k).wait_recv()
         total = t[s, pl.ds(0, piece_rows)]
-        for k in near:
+        for k in last:
             total = total + r1[s, k].astype(F32)
         t[s, pl.ds(0, piece_rows)] = total
         for k in far_first(n):
             l2(s, k).start()
-
-    merge(1)
 
     def l3(s, k):
         mine = v.at[s, part(me[1 - s])]
@@ -350,11 +389,25 @@
         for k in far_first(n):
             l3(s, k).start()
 
+    merge(1)
+
+    def some(cc, s, p, first, count):
+        base = ((cc * 2 + s) * n + p) * piece_rows + first
+        return pl.ds(pl.multiple_of(base, TILE), count)
+
     def l4(s, k):
-        return send(
-            v.at[s, pl.ds(0, piece_rows)], full.at[piece(c, s, me[s])], b4s.at[s, k], b4r.at[s, k],
-            on_axis(s, plus(me[s], k)), grp,
-        )
+        if not tree or k in (1, 2, 6, 7):
+            ref, dst, to = v.at[s, pl.ds(0, piece_rows)], full.at[piece(c, s, me[s])], k
+        elif k in (3, 5):
+            ref = dst = full.at[piece(c, s, plus(me[s], 6 if k == 3 else 2))]
+            to = 1 if k == 3 else 7
+        elif k == 4:
+            ref = dst = full.at[some(c, s, plus(me[s], 6), 0, cut)]
+            to = 2
+        else:
+            ref = dst = full.at[some(c, s, plus(me[s], 2), cut, piece_rows - cut)]
+            to = 6
+        return send(ref, dst, b4s.at[s, k], b4r.at[s, k], on_axis(s, plus(me[s], to)), grp)
 
     def l5(s, k):
         at = full.at[piece(c, s, plus(me[s], k))]
@@ -367,18 +420,27 @@
     for s in (0, 1):
         for k in near:
             l3_in(s, k).wait_recv()
-        for k in far_first(n):
+        for k in ([2, 6, 1, 7] if tree else far_first(n)):
             l4(s, k).start()
         full[piece(c, s, me[s])] = v[s, pl.ds(0, piece_rows)]
         l5(s, 0).start()
 
     def l4_in(s, k):
         at = full.at[piece(c, s, plus(me[s], n - k))]
+        if tree and k == 4:
+            at = full.at[some(c, s, plus(me[s], 4), 0, cut)]
+        elif tree and k == 0:
+            at = full.at[some(c, s, plus(me[s], 4), cut, piece_rows - cut)]
         return send(at, at, b4s.at[s, k], b4r.at[s, k], other, grp)
 
-    for k in near:
+    for k in ([2, 6, 1, 7, 3, 5, 4] if tree else near):
         for s in (0, 1):
             l4_in(s, k).wait_recv()
+            if tree and k == 4:
+                l4_in(s, 0).wait_recv()
+            if tree and k in (2, 6):
+                l4(s, 3 if k == 2 else 5).start()
+                l4(s, 4 if k == 2 else 0).start()
             l5(s, n - k).start()
 
     def finish(arr):
@@ -416,16 +478,17 @@
     for ref, size, first in ((dqb_ref, qkv, 0), (dob_ref, width, qtiles)):
         for j in range(-(-size // LANES)):
             w = min(LANES, size - j * LANES)
-            ref[:, j * LANES:j * LANES + w] = sums[first + j:first + j + 1, :w]
+            ref[j * LANES:j * LANES + w] = sums[first + j, :w]
     for k in range(n):
         for s in (0, 1):
             l0(s, k).wait_send()
             l5(s, k).wait_send()
+            if k or tree:
+                l1(s, k).wait_send()
+                l4(s, k).wait_send()
             if k:
-                l1(s, k).wait_send()
                 l2(s, k).wait_send()
                 l3(s, k).wait_send()
-                l4(s, k).wait_send()
     for arr in (0, 1):
         def done(img, _, arr=arr):
             for j in range(6):
@@ -434,6 +497,16 @@
                 g_copy(arr, img, j).wait_send()
             return 0
         lax.fori_loop(0, slots, done, 0)
+
+
+def store_all(count, *refs):
+    copies = [
+        pltpu.make_async_copy(refs[i], refs[count + i], refs[-1].at[i]) for i in range(count)
+    ]
+    for cp in copies:
+        cp.start()
+    for cp in copies:
+        cp.wait()
 
 
 def local(tokens, cotangent, slot_table, w_qkv, qkv_bias, w_out, out_bias):
@@ -450,8 +523,7 @@
     piece_rows, part_rows, half = nb * TILE, nb2 * TILE, width // 2
     chunks = 2 * slots
     vm = pl.BlockSpec(memory_space=pltpu.VMEM)
-    hbm = pl.BlockSpec(memory_space=pl.ANY)
-    smem = pl.BlockSpec(memory_space=pltpu.SMEM)
+    hbm = pl.BlockSpec(memory_space=pltpu.HBM)
     dma = pltpu.SemaphoreType.DMA
     outs = pl.pallas_call(
         functools.partial(kernel, n, nb, nb2, slots, scale),
@@ -459,19 +531,22 @@
             jax.ShapeDtypeStruct((width, rows), BF16),
             jax.ShapeDtypeStruct((width, rows), BF16),
             jax.ShapeDtypeStruct((qkv, model), BF16),
-            jax.ShapeDtypeStruct((1, qkv), F32),
+            jax.ShapeDtypeStruct((qkv,), F32),
             jax.ShapeDtypeStruct((heads, model), BF16),
-            jax.ShapeDtypeStruct((1, width), F32),
+            jax.ShapeDtypeStruct((width,), F32),
         ),
-        in_specs=[smem, hbm, hbm, hbm, vm, hbm, vm],
+        in_specs=[hbm] * 7,
         out_specs=(vm,) * 6,
         scratch_shapes=[
             pltpu.VMEM((2, slots, model, IMG), BF16),
             pltpu.VMEM((width, rows), BF16),
+            pltpu.SMEM(slot_table.shape[::-1], jnp.int32),
             pltpu.VMEM((qkv, model), BF16),
             pltpu.VMEM((model, qkv), BF16),
             pltpu.VMEM((heads, model), BF16),
             pltpu.VMEM((model, heads), BF16),
+            pltpu.VMEM((qkv,), F32),
+            pltpu.VMEM((width,), F32),
             pltpu.VMEM((qkv, IMG), F32),
             pltpu.VMEM((width, IMG), F32),
             pltpu.VMEM((slots, model, IMG), BF16),
@@ -485,6 +560,7 @@
             pltpu.VMEM((2, n, piece_rows, LANES), F32),
             pltpu.VMEM((2, n, piece_rows, LANES), BF16),
             pltpu.VMEM((2, n, piece_rows, LANES), BF16),
+            pltpu.VMEM((2, 2, piece_rows, LANES), F32),
             pltpu.VMEM((2, n * part_rows, LANES), F32),
             pltpu.VMEM((2, n, part_rows, LANES), F32),
             pltpu.VMEM((2, n * part_rows, LANES), BF16),
@@ -492,14 +568,25 @@
             pltpu.VMEM((chunks, 2, half, IMG), BF16),
             pltpu.VMEM((chunks, 2, half, IMG), BF16),
             pltpu.VMEM((chunks, 2, 2, half, IMG), BF16),
-        ] + [dma((2, n))] * 12 + [dma((chunks, 6))] * 2 + [dma((chunks, 4))] * 2 + [dma((slots + 3,))],
+        ] + [dma((2, n))] * 12 + [dma((chunks, 6))] * 2 + [dma((chunks, 4))] * 2 + [dma((slots + 6,))],
         compiler_params=pltpu.CompilerParams(
             collective_id=0, has_side_effects=True, vmem_limit_bytes=50 * 2**20,
         ),
         cost_estimate=pl.CostEstimate(flops=4 * 10**9, bytes_accessed=10**7, transcendentals=0),
-    )(slot_table.T, tokens.T, cotangent.T, w_qkv.T, qkv_bias.reshape(1, qkv), w_out, out_bias.reshape(1, width))
+    )(*(
+        pltpu.with_memory_space_constraint(a, pltpu.HBM)
+        for a in (slot_table.T, tokens.T, cotangent.T, w_qkv.T, qkv_bias, w_out, out_bias)
+    ))
+    count = len(outs)
+    outs = pl.pallas_call(
+        functools.partial(store_all, count),
+        out_shape=tuple(jax.ShapeDtypeStruct(o.shape, o.dtype) for o in outs),
+        in_specs=[vm] * count,
+        out_specs=(hbm,) * count,
+        scratch_shapes=[dma((count,))],
+    )(*outs)
     layer_out, input_grad, dq, dqb, do, dob = outs
-    return (layer_out.T, input_grad.T, dq.T, dqb.reshape(qkv), do, dob.reshape(width))
+    return (layer_out.T, input_grad.T, dq.T, dqb, do, dob)
 
 
 def solution(mesh):

time: 99.5 us -> 93.5 us (0.940)
  local copies, waits for them, and re-layouts: 8.92 us -> 4.46 us
    pallas_call x1, Pallas kernels: 89 us -> 85.1 us  [local(): pl.pallas_call(functools.partial(kernel, n, nb, nb2, slots, scale), out_s...]
    unnamed x15 -> x12, local copies, waits for them, and re-layouts: 8.23 us -> 4.46 us
    pallas_call x0 -> x1, Pallas kernels: none -> 3.11 us  [local(): pl.pallas_call(functools.partial(store_all, count), out_shape=tuple((jax....]
where the time goes in v4:
time: 93.5 us; the launch traced here: 93.3 us
  Pallas kernels  88.2 us (94%)
  local copies, waits for them, and re-layouts  4.46 us (5%)
    pallas_call x1, Pallas kernels, local(): pl.pallas_call(functools.partial(kernel, n, nb, nb2, slots, scale), out_s...  85.1 us
    unnamed x12, local copies, waits for them, and re-layouts  4.46 us
    pallas_call x1, Pallas kernels, local(): pl.pallas_call(functools.partial(store_all, count), out_shape=tuple((jax....  3.11 us

profile of v4, /device:TPU:1, one launch (start us, length us, event | category | flops | bytes accessed | tf_op | source)
XLA Modules:
  0.0 93.3 jit_solution(7944350597330978896)
XLA Ops:
  0.6 85.1 %shard_map.118 = (bf16[320,640]{1,0:T(8,128)(2,1)S(1)}, bf16[320,640]{1,0:T(8,128)(2,1)S(1)}, bf16[480,1280]{1,0:T(8,128)(2,1)S(1)}, f32[480]{0:T(512)S(1)}, bf1...) custom-call(s32[2,640]{1,0:T(2,128)} %bitcast.13, bf16[320,640]{1,0:T(8,128)(2,1)} %bitcast.9, bf16[320,640]{1,0:T(8,128)(2,1)} %bitcast.10, ...), custom_call_target="tpu_custom_call" | custom-call | flops 4000000000 | bytes 10000000 | tf_op jit(solution)/shard_map/pallas_call | solution.py:528
  85.7 0.0 copy-start
  85.7 1.0 %copy-done = bf16[480,1280]{1,0:T(8,128)(2,1)} copy-done((bf16[480,1280]{1,0:T(8,128)(2,1)}, bf16[480,1280]{1,0:T(8,128)(2,1)S(1)}, u32[]{:S(2)}) %copy-start) | copy-done | bytes 1228824
  86.7 0.0 copy-start.1
  86.7 0.8 copy-done.1
  87.5 0.0 copy-start.2
  87.5 0.7 copy-done.2
  88.3 0.0 copy-start.3
  88.3 0.7 copy-done.3
  89.0 0.0 copy-start.4
  89.0 0.6 copy-done.4
  89.6 0.0 copy-start.5
  89.6 0.6 copy-done.5
  90.2 3.1 %shard_map.119 = (bf16[320,640]{1,0:T(8,128)(2,1)}, bf16[320,640]{1,0:T(8,128)(2,1)}, bf16[480,1280]{1,0:T(8,128)(2,1)}, f32[480]{0:T(512)}, bf16[160,1280]{1,0:T(8,128)(2,1)}, /*index=5*/f32[320]{0:T(512)}) custom-call(bf16[320,640]{1,0:T(8,128)(2,1)} %copy-done.1, bf16[320,640]{1,0:T(8,128)(2,1)} %copy-done.2, bf16[480,1280]{1,0:T(8,128)(2,1)} %copy-done, ...), custom_call_target="tpu_custom_call" | custom-call | tf_op jit(solution)/shard_map/pallas_call | solution.py:581
Async XLA Ops:
  85.7 1.0 %copy-start = (bf16[480,1280]{1,0:T(8,128)(2,1)}, bf16[480,1280]{1,0:T(8,128)(2,1)S(1)}, u32[]{:S(2)}) copy-start(bf16[480,1280]{1,0:T(8,128)(2,1)S(1)} %get-tuple-element.20.refs_2_) | copy-start | bytes 3686404
  86.7 0.8 copy-start.1
  87.5 0.7 copy-start.2
  88.3 0.7 copy-start.3
  89.0 0.6 copy-start.4
  89.6 0.6 copy-start.5

commit v5 on v4

--- a/solution.py
+++ b/solution.py
@@ -13,6 +13,8 @@
 GROUPS = 4
 LANES = 128
 TILE = 16
+STREAMS = 2
+AHEAD = 2
 MESH = pl.DeviceIdType.MESH
 BF16 = jnp.bfloat16
 F32 = jnp.float32
@@ -39,7 +41,7 @@
     tab_ref, x_ref, ct_ref, wq_ref, qb_ref, wo_ref, ob_ref,
     lo_ref, ig_ref, dq_ref, dqb_ref, do_ref, dob_ref,
     gat, ctv, tab, wq, wqn, wo, won, qb, ob, qbb, obb, op, ip, grad, gpf, qsum, osum, gps, mixs,
-    r0, s1, r1, m1, t, r2, v, full, fw, mrg, rcv,
+    r0, s1, r1, m1, t, t2, r2, v, full, fw, mrg, rcv,
     b0s, b0r, b1s, b1r, b2s, b2r, b3s, b3r, b4s, b4r, b5s, b5r,
     xs, xr, gs, gr_sem, ls,
 ):
@@ -90,17 +92,6 @@
     def hi_of(g):
         return pl.ds(pl.multiple_of(g * width + half, TILE), half)
 
-    barrier = pltpu.get_barrier_semaphore()
-    pl.semaphore_signal(barrier, inc=1, device_id=(other, grp), device_id_type=MESH)
-    for axis in (0, 1):
-        for k in range(1, n):
-            pl.semaphore_signal(
-                barrier, inc=1, device_id=(on_axis(axis, plus(me[axis], k)), grp),
-                device_id_type=MESH,
-            )
-    for g in (gr, gl):
-        pl.semaphore_signal(barrier, inc=1, device_id=(dp, g), device_id_type=MESH)
-
     loads = [
         pltpu.make_async_copy(
             x_ref.at[:, i * IMG:(i + 1) * IMG], gat.at[0, i, shard(grp)], ls.at[i]
@@ -113,9 +104,22 @@
     load_tab = pltpu.make_async_copy(tab_ref, tab, ls.at[slots + 3])
     load_qb = pltpu.make_async_copy(qb_ref, qb, ls.at[slots + 4])
     load_ob = pltpu.make_async_copy(ob_ref, ob, ls.at[slots + 5])
+    loads[0].start()
     load_tab.start()
     load_ct.start()
-    for cp in loads:
+
+    barrier = pltpu.get_barrier_semaphore()
+    for g in (gr, gl):
+        pl.semaphore_signal(barrier, inc=1, device_id=(dp, g), device_id_type=MESH)
+    pl.semaphore_signal(barrier, inc=1, device_id=(other, grp), device_id_type=MESH)
+    for axis in (0, 1):
+        for k in range(1, n):
+            pl.semaphore_signal(
+                barrier, inc=1, device_id=(on_axis(axis, plus(me[axis], k)), grp),
+                device_id_type=MESH,
+            )
+
+    for cp in loads[1:]:
         cp.start()
     load_wq.start()
     load_wo.start()
@@ -126,13 +130,9 @@
         lane = lax.broadcasted_iota(jnp.int32, shape, 1)
         return lane < tab[0, dp * slots + img]
 
-    load_tab.wait()
-    load_ct.wait()
-    for i in range(slots):
+    def mask(i):
         rows = ctv[:, i * IMG:(i + 1) * IMG].astype(F32)
         gat[1, i, shard(grp)] = jnp.where(lanes_below(i, rows.shape), rows, 0.0).astype(BF16)
-    for cp in loads:
-        cp.wait()
 
     def g_copy(arr, img, j):
         ch = arr * slots + img
@@ -151,8 +151,8 @@
         ref = gat.at[arr, img, at]
         return send(ref, ref, gs.at[ch, j], gr_sem.at[ch, j], dp, gr)
 
-    def direct(img):
-        for arr in (0, 1):
+    def direct(img, arrs=(0, 1)):
+        for arr in arrs:
             for j in (0, 1):
                 g_copy(arr, img, j).start()
 
@@ -163,8 +163,17 @@
                 g_copy(arr, img, j + 2).start()
 
     pl.semaphore_wait(barrier, 1 + 2 * (n - 1) + 2)
-    direct(0)
-    direct(1)
+    loads[0].wait()
+    direct(0, (0,))
+    load_tab.wait()
+    load_ct.wait()
+    mask(0)
+    direct(0, (1,))
+    for i in range(1, slots):
+        loads[i].wait()
+        mask(i)
+        if i < AHEAD:
+            direct(i)
 
     grad[...] = jnp.zeros(grad.shape, F32)
     qsum[...] = jnp.zeros(qsum.shape, F32)
@@ -180,7 +189,13 @@
         won[j * LANES:(j + 1) * LANES] = wo[:, j * LANES:(j + 1) * LANES].T
     forward(0)
 
+    def halves_in(arr, img):
+        for j in (2, 3):
+            g_in(arr, img, j).wait_recv()
+
     def image_grads(img):
+        halves_in(0, img)
+        halves_in(1, img)
         proj = (dot(wq[...], gat[0, img]) + qbb[...]).astype(BF16)
         gmix = dot(wo[...], gat[1, img]).astype(BF16)
         for h in range(heads // HD):
@@ -188,7 +203,6 @@
             q = proj[at:at + HD]
             k = proj[at + HD:at + 2 * HD]
             val = proj[at + 2 * HD:at + 3 * HD]
-            gm = gmix[h * HD:(h + 1) * HD]
             scores = dot_tn(k, q) * score_scale
             row = lax.broadcasted_iota(jnp.int32, scores.shape, 0)
             scores = jnp.where(row < tab[0, dp * slots + img], scores, -1e30)
@@ -196,6 +210,7 @@
             probs = ex / jnp.sum(ex, axis=0, keepdims=True)
             probs_b = probs.astype(BF16)
             mixs[h * HD:(h + 1) * HD] = dot(val, probs_b).astype(BF16)
+            gm = gmix[h * HD:(h + 1) * HD]
             gprobs = dot_tn(val, gm)
             inner = jnp.sum(probs * gprobs, axis=0, keepdims=True)
             gscores = (probs * (gprobs - inner) * score_scale).astype(BF16)
@@ -220,17 +235,14 @@
         ip[img] = dot(wqn[...], gps[...]).astype(BF16)
 
     def image(img, _):
-        @pl.when(img + 2 < slots)
+        @pl.when(img + AHEAD < slots)
         def _():
-            direct(img + 2)
+            direct(img + AHEAD)
 
         @pl.when(img + 1 < slots)
         def _():
             forward(img + 1)
 
-        for arr in (0, 1):
-            for j in (2, 3):
-                g_in(arr, img, j).wait_recv()
         image_grads(img)
 
         @pl.when(img + 1 < slots)
@@ -253,16 +265,16 @@
     order = far_first(n) + [0]
 
     def piece(cc, s, p):
-        return pl.ds(pl.multiple_of(((cc * 2 + s) * n + p) * piece_rows, TILE), piece_rows)
+        return pl.ds(pl.multiple_of(((cc * STREAMS + s) * n + p) * piece_rows, TILE), piece_rows)
 
     def l0(s, k):
-        p = plus(me[s], k)
+        p = plus(me[s % 2], k)
         return send(
             grad.at[piece(1 - c, s, p)], r0.at[s, p], b0s.at[s, k], b0r.at[s, k], other, grp
         )
 
     for k in order:
-        for s in (0, 1):
+        for s in range(STREAMS):
             l0(s, k).start()
     image_parts(slots - 1)
 
@@ -279,6 +291,19 @@
         )[j]()
         return send(ref, dst, xs.at[ch, j], xr.at[ch, j], dp, to)
 
+    def merge(arr):
+        def step(img, _):
+            ch = arr * slots + img
+            src = (op, ip)[arr]
+            x_copy(arr, img, 0).wait_recv()
+            mrg[ch, 0] = (src[img, lo_of(gr)].astype(F32) + fw[ch, 0].astype(F32)).astype(BF16)
+            x_copy(arr, img, 4).start()
+            x_copy(arr, img, 1).wait_recv()
+            mrg[ch, 1] = (src[img, hi_of(gl)].astype(F32) + fw[ch, 1].astype(F32)).astype(BF16)
+            x_copy(arr, img, 5).start()
+            return 0
+        lax.fori_loop(0, slots, step, 0)
+
     for arr in (0, 1):
         def raw(img, _, arr=arr):
             for j in range(4):
@@ -300,12 +325,12 @@
             ref, dst, to = s1.at[s, 4, head_rows], r1.at[s, 4, head_rows], 2
         elif tree and k == 0:
             ref, dst, to = s1.at[s, 4, tail_rows], r1.at[s, 4, tail_rows], 6
-        return send(ref, dst, b1s.at[s, k], b1r.at[s, k], on_axis(s, plus(me[s], to)), grp)
+        return send(ref, dst, b1s.at[s, k], b1r.at[s, k], on_axis(s % 2, plus(me[s % 2], to)), grp)
 
     for k in order:
-        for s in (0, 1):
+        for s in range(STREAMS):
             l0(s, k).wait_recv()
-            p = plus(me[s], k)
+            p = plus(me[s % 2], k)
             total = grad[piece(c, s, p)] + r0[s, p]
             if tree and k in (2, 6):
                 m1[s, k // 4] = total
@@ -319,22 +344,10 @@
                 rest = part_rows * n - piece_rows
                 if rest:
                     t[s, pl.ds(piece_rows, rest)] = jnp.zeros((rest, LANES), F32)
-
-    def merge(arr):
-        def step(img, _):
-            ch = arr * slots + img
-            src = (op, ip)[arr]
-            x_copy(arr, img, 0).wait_recv()
-            mrg[ch, 0] = (src[img, lo_of(gr)].astype(F32) + fw[ch, 0].astype(F32)).astype(BF16)
-            x_copy(arr, img, 4).start()
-            x_copy(arr, img, 1).wait_recv()
-            mrg[ch, 1] = (src[img, hi_of(gl)].astype(F32) + fw[ch, 1].astype(F32)).astype(BF16)
-            x_copy(arr, img, 5).start()
-            return 0
-        lax.fori_loop(0, slots, step, 0)
+                    t2[s, pl.ds(piece_rows, rest)] = jnp.zeros((rest, LANES), BF16)
 
     if tree:
-        for s in (0, 1):
+        for s in range(STREAMS):
             l1(s, 3).wait_recv()
             l1(s, 4).wait_recv()
             s1[s, 2, head_rows] = (
@@ -350,91 +363,92 @@
             ).astype(BF16)
             l1(s, 6).start()
 
-    merge(0)
-
     def part(q):
         return pl.ds(pl.multiple_of(q * part_rows, TILE), part_rows)
 
     def l2(s, k):
-        q = plus(me[1 - s], k)
+        q = plus(me[1 - s % 2], k)
         return send(
-            t.at[s, part(q)], r2.at[s, k], b2s.at[s, k], b2r.at[s, k], on_axis(1 - s, q), grp,
+            t2.at[s, part(q)], r2.at[s, k], b2s.at[s, k], b2r.at[s, k], on_axis(1 - s % 2, q), grp,
         )
 
     near = list(reversed(far_first(n)))
     last = [1, 7, 2, 6] if tree else near
-    for s in (0, 1):
+    for s in range(STREAMS):
         for k in last:
             l1(s, k).wait_recv()
         total = t[s, pl.ds(0, piece_rows)]
         for k in last:
             total = total + r1[s, k].astype(F32)
         t[s, pl.ds(0, piece_rows)] = total
+        t2[s, pl.ds(0, piece_rows)] = total.astype(BF16)
         for k in far_first(n):
             l2(s, k).start()
 
     def l3(s, k):
-        mine = v.at[s, part(me[1 - s])]
+        mine = v.at[s, part(me[1 - s % 2])]
         return send(
-            mine, mine, b3s.at[s, k], b3r.at[s, k], on_axis(1 - s, plus(me[1 - s], k)), grp,
+            mine, mine, b3s.at[s, k], b3r.at[s, k], on_axis(1 - s % 2, plus(me[1 - s % 2], k)), grp,
         )
 
-    for s in (0, 1):
+    for s in range(STREAMS):
         for k in near:
             l2(s, k).wait_recv()
-        total = t[s, part(me[1 - s])]
+        total = t[s, part(me[1 - s % 2])]
         for k in near:
-            total = total + r2[s, k]
-        v[s, part(me[1 - s])] = (total * scale).astype(BF16)
+            total = total + r2[s, k].astype(F32)
+        v[s, part(me[1 - s % 2])] = (total * scale).astype(BF16)
         for k in far_first(n):
             l3(s, k).start()
 
-    merge(1)
+    merge(0)
 
     def some(cc, s, p, first, count):
-        base = ((cc * 2 + s) * n + p) * piece_rows + first
+        base = ((cc * STREAMS + s) * n + p) * piece_rows + first
         return pl.ds(pl.multiple_of(base, TILE), count)
 
     def l4(s, k):
         if not tree or k in (1, 2, 6, 7):
-            ref, dst, to = v.at[s, pl.ds(0, piece_rows)], full.at[piece(c, s, me[s])], k
+            ref, dst, to = v.at[s, pl.ds(0, piece_rows)], full.at[piece(c, s, me[s % 2])], k
         elif k in (3, 5):
-            ref = dst = full.at[piece(c, s, plus(me[s], 6 if k == 3 else 2))]
+            ref = dst = full.at[piece(c, s, plus(me[s % 2], 6 if k == 3 else 2))]
             to = 1 if k == 3 else 7
         elif k == 4:
-            ref = dst = full.at[some(c, s, plus(me[s], 6), 0, cut)]
+            ref = dst = full.at[some(c, s, plus(me[s % 2], 6), 0, cut)]
             to = 2
         else:
-            ref = dst = full.at[some(c, s, plus(me[s], 2), cut, piece_rows - cut)]
+            ref = dst = full.at[some(c, s, plus(me[s % 2], 2), cut, piece_rows - cut)]
             to = 6
-        return send(ref, dst, b4s.at[s, k], b4r.at[s, k], on_axis(s, plus(me[s], to)), grp)
+        return send(ref, dst, b4s.at[s, k], b4r.at[s, k], on_axis(s % 2, plus(me[s % 2], to)), grp)
 
     def l5(s, k):
-        at = full.at[piece(c, s, plus(me[s], k))]
+        at = full.at[piece(c, s, plus(me[s % 2], k))]
         return send(at, at, b5s.at[s, k], b5r.at[s, k], other, grp)
 
     def l3_in(s, k):
-        at = v.at[s, part(plus(me[1 - s], n - k))]
+        at = v.at[s, part(plus(me[1 - s % 2], n - k))]
         return send(at, at, b3s.at[s, k], b3r.at[s, k], other, grp)
 
-    for s in (0, 1):
+    for s in range(STREAMS):
         for k in near:
             l3_in(s, k).wait_recv()
         for k in ([2, 6, 1, 7] if tree else far_first(n)):
             l4(s, k).start()
-        full[piece(c, s, me[s])] = v[s, pl.ds(0, piece_rows)]
+        full[piece(c, s, me[s % 2])] = v[s, pl.ds(0, piece_rows)]
         l5(s, 0).start()
 
+    merge(1)
+
     def l4_in(s, k):
-        at = full.at[piece(c, s, plus(me[s], n - k))]
+        at = full.at[piece(c, s, plus(me[s % 2], n - k))]
         if tree and k == 4:
-            at = full.at[some(c, s, plus(me[s], 4), 0, cut)]
+            at = full.at[some(c, s, plus(me[s % 2], 4), 0, cut)]
         elif tree and k == 0:
-            at = full.at[some(c, s, plus(me[s], 4), cut, piece_rows - cut)]
+            at = full.at[some(c, s, plus(me[s % 2], 4), cut, piece_rows - cut)]
         return send(at, at, b4s.at[s, k], b4r.at[s, k], other, grp)
 
     for k in ([2, 6, 1, 7, 3, 5, 4] if tree else near):
-        for s in (0, 1):
+        for s in range(STREAMS):
             l4_in(s, k).wait_recv()
             if tree and k == 4:
                 l4_in(s, 0).wait_recv()
@@ -464,11 +478,11 @@
     finish(1)
 
     def l5_in(s, k):
-        at = full.at[piece(1 - c, s, plus(me[s], k))]
+        at = full.at[piece(1 - c, s, plus(me[s % 2], k))]
         return send(at, at, b5s.at[s, k], b5r.at[s, k], other, grp)
 
     for k in range(n):
-        for s in (0, 1):
+        for s in range(STREAMS):
             l5_in(s, k).wait_recv()
     for j in range(tiles):
         at = j * both
@@ -480,7 +494,7 @@
             w = min(LANES, size - j * LANES)
             ref[j * LANES:j * LANES + w] = sums[first + j, :w]
     for k in range(n):
-        for s in (0, 1):
+        for s in range(STREAMS):
             l0(s, k).wait_send()
             l5(s, k).wait_send()
             if k or tree:
@@ -518,7 +532,7 @@
     n = math.isqrt(dp_count // 2)
     scale = 1.0 / math.sqrt(dp_count * slots * IMG)
     used = (qkv + heads) // TILE * (model // LANES) + 1
-    nb = -(-used // (4 * n))
+    nb = -(-used // (2 * STREAMS * n))
     nb2 = -(-nb // n)
     piece_rows, part_rows, half = nb * TILE, nb2 * TILE, width // 2
     chunks = 2 * slots
@@ -551,24 +565,25 @@
             pltpu.VMEM((width, IMG), F32),
             pltpu.VMEM((slots, model, IMG), BF16),
             pltpu.VMEM((slots, model, IMG), BF16),
-            pltpu.VMEM((4 * n * piece_rows, LANES), F32),
+            pltpu.VMEM((2 * STREAMS * n * piece_rows, LANES), F32),
             pltpu.VMEM((qkv, IMG), F32),
             pltpu.VMEM((qkv, IMG), F32),
             pltpu.VMEM((width, IMG), F32),
             pltpu.VMEM((qkv, IMG), BF16),
             pltpu.VMEM((heads, IMG), BF16),
-            pltpu.VMEM((2, n, piece_rows, LANES), F32),
-            pltpu.VMEM((2, n, piece_rows, LANES), BF16),
-            pltpu.VMEM((2, n, piece_rows, LANES), BF16),
-            pltpu.VMEM((2, 2, piece_rows, LANES), F32),
-            pltpu.VMEM((2, n * part_rows, LANES), F32),
-            pltpu.VMEM((2, n, part_rows, LANES), F32),
-            pltpu.VMEM((2, n * part_rows, LANES), BF16),
-            pltpu.VMEM((4 * n * piece_rows, LANES), BF16),
+            pltpu.VMEM((STREAMS, n, piece_rows, LANES), F32),
+            pltpu.VMEM((STREAMS, n, piece_rows, LANES), BF16),
+            pltpu.VMEM((STREAMS, n, piece_rows, LANES), BF16),
+            pltpu.VMEM((STREAMS, 2, piece_rows, LANES), F32),
+            pltpu.VMEM((STREAMS, n * part_rows, LANES), F32),
+            pltpu.VMEM((STREAMS, n * part_rows, LANES), BF16),
+            pltpu.VMEM((STREAMS, n, part_rows, LANES), BF16),
+            pltpu.VMEM((STREAMS, n * part_rows, LANES), BF16),
+            pltpu.VMEM((2 * STREAMS * n * piece_rows, LANES), BF16),
             pltpu.VMEM((chunks, 2, half, IMG), BF16),
             pltpu.VMEM((chunks, 2, half, IMG), BF16),
             pltpu.VMEM((chunks, 2, 2, half, IMG), BF16),
-        ] + [dma((2, n))] * 12 + [dma((chunks, 6))] * 2 + [dma((chunks, 4))] * 2 + [dma((slots + 6,))],
+        ] + [dma((STREAMS, n))] * 12 + [dma((chunks, 6))] * 2 + [dma((chunks, 4))] * 2 + [dma((slots + 6,))],
         compiler_params=pltpu.CompilerParams(
             collective_id=0, has_side_effects=True, vmem_limit_bytes=50 * 2**20,
         ),
@@ -584,7 +599,8 @@
         in_specs=[vm] * count,
         out_specs=(hbm,) * count,
         scratch_shapes=[dma((count,))],
-    )(*outs)
+        compiler_params=pltpu.CompilerParams(vmem_limit_bytes=8 * 2**20),
+    )(*(pltpu.with_memory_space_constraint(o, pltpu.VMEM) for o in outs))
     layer_out, input_grad, dq, dqb, do, dob = outs
     return (layer_out.T, input_grad.T, dq.T, dqb, do, dob)
 

time: 93.5 us -> 86.9 us (0.929)
  local copies, waits for them, and re-layouts: 4.46 us -> 0 us
  Pallas kernels: 88.2 us -> 86.2 us
    unnamed x12 -> x0, local copies, waits for them, and re-layouts: 4.46 us -> none
    pallas_call x1, Pallas kernels: 3.11 us -> 1.49 us  [local(): pl.pallas_call(functools.partial(store_all, count), out_shape=tuple((jax....]
where the time goes in v5:
time: 86.9 us; the launch traced here: 86.8 us
  Pallas kernels  86.2 us (99%)
    pallas_call x1, Pallas kernels, local(): pl.pallas_call(functools.partial(kernel, n, nb, nb2, slots, scale), out_s...  84.7 us

profile of v5, /device:TPU:1, one launch (start us, length us, event | category | flops | bytes accessed | tf_op | source)
XLA Modules:
  0.0 86.8 jit_solution(3086826354087807898)
XLA Ops:
  0.6 84.7 %shard_map.118 = (bf16[320,640]{1,0:T(8,128)(2,1)S(1)}, bf16[320,640]{1,0:T(8,128)(2,1)S(1)}, bf16[480,1280]{1,0:T(8,128)(2,1)S(1)}, f32[480]{0:T(512)S(1)}, bf1...) custom-call(s32[2,640]{1,0:T(2,128)} %bitcast.13, bf16[320,640]{1,0:T(8,128)(2,1)} %bitcast.9, bf16[320,640]{1,0:T(8,128)(2,1)} %bitcast.10, ...), custom_call_target="tpu_custom_call" | custom-call | flops 4000000000 | bytes 10000000 | tf_op jit(solution)/shard_map/pallas_call | solution.py:542
  85.3 1.5 %shard_map.119 = (bf16[320,640]{1,0:T(8,128)(2,1)}, bf16[320,640]{1,0:T(8,128)(2,1)}, bf16[480,1280]{1,0:T(8,128)(2,1)}, f32[480]{0:T(512)}, bf16[160,1280]{1,0:T(8,128)(2,1)}, /*index=5*/f32[320]{0:T(512)}) custom-call(bf16[320,640]{1,0:T(8,128)(2,1)S(1)} %get-tuple-element.18.refs_0_, bf16[320,640]{1,0:T(8,128)(2,1)S(1)} %get-tuple-element.19.refs_1_, ...), custom_call_target="tpu_custom_call" | custom-call | tf_op jit(solution)/shard_map/pallas_call | solution.py:596

commit v6 on v5

--- a/solution.py
+++ b/solution.py
@@ -41,7 +41,7 @@
     tab_ref, x_ref, ct_ref, wq_ref, qb_ref, wo_ref, ob_ref,
     lo_ref, ig_ref, dq_ref, dqb_ref, do_ref, dob_ref,
     gat, ctv, tab, wq, wqn, wo, won, qb, ob, qbb, obb, op, ip, grad, gpf, qsum, osum, gps, mixs,
-    r0, s1, r1, m1, t, t2, r2, v, full, fw, mrg, rcv,
+    r0, s1, r1, m1, t, r2, v, full, fw, mrg, rcv,
     b0s, b0r, b1s, b1r, b2s, b2r, b3s, b3r, b4s, b4r, b5s, b5r,
     xs, xr, gs, gr_sem, ls,
 ):
@@ -311,6 +311,20 @@
             return 0
         lax.fori_loop(0, slots, raw, 0)
 
+    def x_sent(first, last):
+        for arr in (0, 1):
+            def step(img, _, arr=arr):
+                for j in range(first, last):
+                    x_copy(arr, img, j).wait_send()
+                return 0
+            lax.fori_loop(0, slots, step, 0)
+
+    def g_sent(img, _):
+        for arr in (0, 1):
+            for j in range(4):
+                g_copy(arr, img, j).wait_send()
+        return 0
+
     tree = n == 8
     cut = nb // 2 * TILE
     head_rows, tail_rows = pl.ds(0, cut), pl.ds(cut, piece_rows - cut)
@@ -344,7 +358,6 @@
                 rest = part_rows * n - piece_rows
                 if rest:
                     t[s, pl.ds(piece_rows, rest)] = jnp.zeros((rest, LANES), F32)
-                    t2[s, pl.ds(piece_rows, rest)] = jnp.zeros((rest, LANES), BF16)
 
     if tree:
         for s in range(STREAMS):
@@ -363,13 +376,18 @@
             ).astype(BF16)
             l1(s, 6).start()
 
+    lax.fori_loop(0, slots, g_sent, 0)
+    for k in order:
+        for s in range(STREAMS):
+            l0(s, k).wait_send()
+
     def part(q):
         return pl.ds(pl.multiple_of(q * part_rows, TILE), part_rows)
 
     def l2(s, k):
         q = plus(me[1 - s % 2], k)
         return send(
-            t2.at[s, part(q)], r2.at[s, k], b2s.at[s, k], b2r.at[s, k], on_axis(1 - s % 2, q), grp,
+            t.at[s, part(q)], r2.at[s, k], b2s.at[s, k], b2r.at[s, k], on_axis(1 - s % 2, q), grp,
         )
 
     near = list(reversed(far_first(n)))
@@ -381,7 +399,6 @@
         for k in last:
             total = total + r1[s, k].astype(F32)
         t[s, pl.ds(0, piece_rows)] = total
-        t2[s, pl.ds(0, piece_rows)] = total.astype(BF16)
         for k in far_first(n):
             l2(s, k).start()
 
@@ -396,7 +413,7 @@
             l2(s, k).wait_recv()
         total = t[s, part(me[1 - s % 2])]
         for k in near:
-            total = total + r2[s, k].astype(F32)
+            total = total + r2[s, k]
         v[s, part(me[1 - s % 2])] = (total * scale).astype(BF16)
         for k in far_first(n):
             l3(s, k).start()
@@ -438,6 +455,15 @@
         l5(s, 0).start()
 
     merge(1)
+
+    for k in range(n):
+        for s in range(STREAMS):
+            if k or tree:
+                l1(s, k).wait_send()
+            if k:
+                l2(s, k).wait_send()
+                l3(s, k).wait_send()
+    x_sent(0, 4)
 
     def l4_in(s, k):
         at = full.at[piece(c, s, plus(me[s % 2], n - k))]
@@ -475,7 +501,6 @@
         lax.fori_loop(0, slots, step, 0)
 
     finish(0)
-    finish(1)
 
     def l5_in(s, k):
         at = full.at[piece(1 - c, s, plus(me[s % 2], k))]
@@ -493,24 +518,13 @@
         for j in range(-(-size // LANES)):
             w = min(LANES, size - j * LANES)
             ref[j * LANES:j * LANES + w] = sums[first + j, :w]
+    finish(1)
     for k in range(n):
         for s in range(STREAMS):
-            l0(s, k).wait_send()
             l5(s, k).wait_send()
             if k or tree:
-                l1(s, k).wait_send()
                 l4(s, k).wait_send()
-            if k:
-                l2(s, k).wait_send()
-                l3(s, k).wait_send()
-    for arr in (0, 1):
-        def done(img, _, arr=arr):
-            for j in range(6):
-                x_copy(arr, img, j).wait_send()
-            for j in range(4):
-                g_copy(arr, img, j).wait_send()
-            return 0
-        lax.fori_loop(0, slots, done, 0)
+    x_sent(4, 6)
 
 
 def store_all(count, *refs):
@@ -576,8 +590,7 @@
             pltpu.VMEM((STREAMS, n, piece_rows, LANES), BF16),
             pltpu.VMEM((STREAMS, 2, piece_rows, LANES), F32),
             pltpu.VMEM((STREAMS, n * part_rows, LANES), F32),
-            pltpu.VMEM((STREAMS, n * part_rows, LANES), BF16),
-            pltpu.VMEM((STREAMS, n, part_rows, LANES), BF16),
+            pltpu.VMEM((STREAMS, n, part_rows, LANES), F32),
             pltpu.VMEM((STREAMS, n * part_rows, LANES), BF16),
             pltpu.VMEM((2 * STREAMS * n * piece_rows, LANES), BF16),
             pltpu.VMEM((chunks, 2, half, IMG), BF16),

time: 86.9 us -> 87.2 us (level)
  no operation moved by 1% of the time
where the time goes in v6:
time: 87.2 us; the launch traced here: 87 us
  Pallas kernels  86.4 us (99%)
    pallas_call x1, Pallas kernels, local(): pl.pallas_call(functools.partial(kernel, n, nb, nb2, slots, scale), out_s...  84.9 us

profile of v6, /device:TPU:1, one launch (start us, length us, event | category | flops | bytes accessed | tf_op | source)
XLA Modules:
  0.0 87.0 jit_solution(11198564229843803264)
XLA Ops:
  0.6 84.9 %shard_map.118 = (bf16[320,640]{1,0:T(8,128)(2,1)S(1)}, bf16[320,640]{1,0:T(8,128)(2,1)S(1)}, bf16[480,1280]{1,0:T(8,128)(2,1)S(1)}, f32[480]{0:T(512)S(1)}, bf1...) custom-call(s32[2,640]{1,0:T(2,128)} %bitcast.13, bf16[320,640]{1,0:T(8,128)(2,1)} %bitcast.9, bf16[320,640]{1,0:T(8,128)(2,1)} %bitcast.10, ...), custom_call_target="tpu_custom_call" | custom-call | flops 4000000000 | bytes 10000000 | tf_op jit(solution)/shard_map/pallas_call | solution.py:556
  85.6 1.5 %shard_map.119 = (bf16[320,640]{1,0:T(8,128)(2,1)}, bf16[320,640]{1,0:T(8,128)(2,1)}, bf16[480,1280]{1,0:T(8,128)(2,1)}, f32[480]{0:T(512)}, bf16[160,1280]{1,0:T(8,128)(2,1)}, /*index=5*/f32[320]{0:T(512)}) custom-call(bf16[320,640]{1,0:T(8,128)(2,1)S(1)} %get-tuple-element.18.refs_0_, bf16[320,640]{1,0:T(8,128)(2,1)S(1)} %get-tuple-element.19.refs_1_, ...), custom_call_target="tpu_custom_call" | custom-call | tf_op jit(solution)/shard_map/pallas_call | solution.py:609

commit v7 on v6

--- a/solution.py
+++ b/solution.py
@@ -237,11 +237,15 @@
     def image(img, _):
         @pl.when(img + AHEAD < slots)
         def _():
-            direct(img + AHEAD)
+            direct(img + AHEAD, (0,))
 
         @pl.when(img + 1 < slots)
         def _():
             forward(img + 1)
+
+        @pl.when(img + AHEAD < slots)
+        def _():
+            direct(img + AHEAD, (1,))
 
         image_grads(img)
 

time: 87.2 us -> 86.7 us (level)
  no operation moved by 1% of the time
where the time goes in v7:
time: 86.7 us; the launch traced here: 86.6 us
  Pallas kernels  85.9 us (99%)
    pallas_call x1, Pallas kernels, local(): pl.pallas_call(functools.partial(kernel, n, nb, nb2, slots, scale), out_s...  84.4 us

profile of v7, /device:TPU:1, one launch (start us, length us, event | category | flops | bytes accessed | tf_op | source)
XLA Modules:
  0.0 86.6 jit_solution(12269305771945616493)
XLA Ops:
  0.6 84.4 %shard_map.118 = (bf16[320,640]{1,0:T(8,128)(2,1)S(1)}, bf16[320,640]{1,0:T(8,128)(2,1)S(1)}, bf16[480,1280]{1,0:T(8,128)(2,1)S(1)}, f32[480]{0:T(512)S(1)}, bf1...) custom-call(s32[2,640]{1,0:T(2,128)} %bitcast.13, bf16[320,640]{1,0:T(8,128)(2,1)} %bitcast.9, bf16[320,640]{1,0:T(8,128)(2,1)} %bitcast.10, ...), custom_call_target="tpu_custom_call" | custom-call | flops 4000000000 | bytes 10000000 | tf_op jit(solution)/shard_map/pallas_call | solution.py:560
  85.1 1.5 %shard_map.119 = (bf16[320,640]{1,0:T(8,128)(2,1)}, bf16[320,640]{1,0:T(8,128)(2,1)}, bf16[480,1280]{1,0:T(8,128)(2,1)}, f32[480]{0:T(512)}, bf16[160,1280]{1,0:T(8,128)(2,1)}, /*index=5*/f32[320]{0:T(512)}) custom-call(bf16[320,640]{1,0:T(8,128)(2,1)S(1)} %get-tuple-element.18.refs_0_, bf16[320,640]{1,0:T(8,128)(2,1)S(1)} %get-tuple-element.19.refs_1_, ...), custom_call_target="tpu_custom_call" | custom-call | tf_op jit(solution)/shard_map/pallas_call | solution.py:613
